TPU v7x, 128 devices: a whole 4x4x4 slice. The times are simulated.
128 devices in a mesh: gx: 32 (over y, z, core), gy: 4 (over x).
Axes of the slice: x: 4, y: 4, z: 4, core: 2. Of those that a mesh axis runs over, the one named last changes fastest.
Arguments:
- beta: float32 [512, 256, 256], P('gx', 'gy'), may hold values from 0.25 to 4
- jump_rhs: float32 [262144], P(('gx', 'gy')), may hold values from -15 to 15
- stiffness: float32 [262144], P(('gx', 'gy')), may hold values from 0.1 to 1
- spread_weight: float32 [262144], P(('gx', 'gy')), may hold values from 0.5 to 1.5
- grid_owner: int32 [262144, 1], P(('gx', 'gy')), may hold values from 0 to 127; in each aligned block of 2048 rows (0 to 2047, 2048 to 4095, ...) at most 32 rows name the same one
- cell_index: int32 [262144], P(('gx', 'gy')), may hold values from 0 to 262143
- block_count: int32 [128], P(('gx', 'gy')), may hold values from 8 to 16, as said below
Outputs:
- solution: float32 [262144], P(('gx', 'gy'))
- residual: float32 [262144], P(('gx', 'gy'))
Inputs may be any that keep to these rules, and one draw needn't show every extreme that they name: `grid_owner`: among the 2048 slots of each owner no device is named more than 32 times, and some device exactly 32 times. `cell_index`: cells are numbered with x slowest, then y, then z, inside the tile of 16 x 64 x 256 cells. `block_count`: slots in later blocks of an owner are padding; some owner has all 16 blocks live.
All inputs are finite; a program needn't handle non-finite values.
Results may differ from a plain program's by a relative error of at most 0.0003.
Values sent between devices are 32-bit elements; how exact they have to be, the bound alone decides.
A program may use at most 64 MiB of HBM per device.

v0:
```python
import jax
import jax.numpy as jnp
from jax import lax
from jax.sharding import PartitionSpec as P

BLOCK = 128
CHEB = 6
ITERS = 2


SHIFT = 0.01
THETA = 1.025
DELTA = 0.975
SIGMA = THETA / DELTA
EPS = 1e-06


def padded_2(x, sides, width):
    for axis, dim in sides:
        count, length = (lax.axis_size(axis), x.shape[dim])
        up = [(i, (i + 1) % count) for i in range(count - 1)]
        down = [(j, i) for i, j in up]
        last = lax.slice_in_dim(x, length - width, length, axis=dim)
        leading = lax.slice_in_dim(x, 0, width, axis=dim)
        before = lax.ppermute(last, axis, up)
        after = lax.ppermute(leading, axis, down)
        x = jnp.concatenate([before, x, after], axis=dim)
    return x


def harmonic(left, right):
    total = left + right
    return 2.0 * left * right / jnp.where(total > 0, total, 1.0)


def faces(beta_pad):
    padded = jnp.pad(beta_pad, ((0, 0), (0, 0), (1, 1)))
    coef_x = harmonic(padded[:-1, 1:-1, 1:-1], padded[1:, 1:-1, 1:-1])
    coef_y = harmonic(padded[1:-1, :-1, 1:-1], padded[1:-1, 1:, 1:-1])
    coef_z = harmonic(padded[1:-1, 1:-1, :-1], padded[1:-1, 1:-1, 1:])
    diagonal = (
        SHIFT
        + coef_x[:-1]
        + coef_x[1:]
        + coef_y[:, :-1]
        + coef_y[:, 1:]
        + coef_z[:, :, :-1]
        + coef_z[:, :, 1:]
    )
    return (coef_x, coef_y, coef_z, diagonal)


def operate(field_pad, coef_x, coef_y, coef_z, diagonal):
    padded = jnp.pad(field_pad, ((0, 0), (0, 0), (1, 1)))
    centre = padded[1:-1, 1:-1, 1:-1]
    beside = coef_x[1:] * padded[2:, 1:-1, 1:-1] + coef_x[:-1] * padded[:-2, 1:-1, 1:-1]
    beside = (
        beside + coef_y[:, 1:] * padded[1:-1, 2:, 1:-1] + coef_y[:, :-1] * padded[1:-1, :-2, 1:-1]
    )
    beside = (
        beside
        + coef_z[:, :, 1:] * padded[1:-1, 1:-1, 2:]
        + coef_z[:, :, :-1] * padded[1:-1, 1:-1, :-2]
    )
    return diagonal * centre - beside


def chebyshev_rim(source, coefs):
    coef_x, coef_y, coef_z, diagonal = coefs
    ratio = 1.0 / SIGMA
    update = source / (THETA * diagonal)
    field = update
    for sweep in range(CHEB - 1):
        field_pad = padded_2(field, (("gx", 0), ("gy", 1)), 1)
        image = operate(field_pad, coef_x, coef_y, coef_z, diagonal)
        ratio_next = 1.0 / (2.0 * SIGMA - ratio)
        update = (
            ratio_next * ratio * update + 2.0 * ratio_next / DELTA * (source - image) / diagonal
        )
        field = field + update
        ratio = ratio_next
    return field


def least_squares(start, columns):
    count = len(columns)
    targets = [start] + [start * 0.0 for unused in range(count)]
    cosines = []
    sines = []
    upper = []
    for outer in range(count):
        column = list(columns[outer])
        for inner in range(outer):
            first = cosines[inner] * column[inner] + sines[inner] * column[inner + 1]
            second = -sines[inner] * column[inner] + cosines[inner] * column[inner + 1]
            column[inner] = first
            column[inner + 1] = second
        radius = jnp.sqrt(column[outer] * column[outer] + column[outer + 1] * column[outer + 1])
        cosine = column[outer] / radius
        sine = column[outer + 1] / radius
        column[outer] = radius
        targets[outer + 1] = -sine * targets[outer]
        targets[outer] = cosine * targets[outer]
        cosines.append(cosine)
        sines.append(sine)
        upper.append(column)
    coeffs = [None] * count
    for outer in reversed(range(count)):
        total = targets[outer]
        for later in range(outer + 1, count):
            total = total - upper[later][outer] * coeffs[later]
        coeffs[outer] = total / upper[outer][outer]
    return coeffs


def length(vector):
    return jnp.sqrt(lax.psum(jnp.sum(vector * vector), ("gx", "gy")) + EPS)


def on_device(beta, jump_rhs, stiffness, spread_weight, grid_owner, cell_index, block_count):
    size_x, size_y, size_z = beta.shape
    owners = lax.axis_size("gx") * lax.axis_size("gy")
    points = jump_rhs.shape[0]
    blocks = points // BLOCK
    capacity = 2 * points // owners
    columns_xy = size_x * size_y
    live = jnp.arange(points, dtype=jnp.int32) // BLOCK < block_count[0]
    target = grid_owner[:, 0]
    onehot = (target.reshape(blocks, BLOCK, 1) == jnp.arange(owners, dtype=jnp.int32)).astype(
        jnp.float32
    )
    lower = (jnp.arange(BLOCK)[None, :] < jnp.arange(BLOCK)[:, None]).astype(jnp.float32)
    within = jnp.einsum("ij,bjd->bid", lower, onehot, precision=lax.Precision.HIGHEST)
    totals = jnp.sum(onehot, axis=1)
    offsets = jnp.cumsum(totals, axis=0) - totals
    rank = (
        jnp.sum((within + offsets[:, None, :]) * onehot, axis=-1).reshape(points).astype(jnp.int32)
    )
    slot_of = target * capacity + rank
    slot_table = (
        slot_of[:, None] == jnp.arange(owners * capacity, dtype=jnp.int32)[None, :]
    ).astype(jnp.float32)
    slots = jnp.zeros((owners, capacity), jnp.int32).at[target, rank].set(cell_index)
    arrived = lax.all_to_all(slots, ("gx", "gy"), split_axis=0, concat_axis=0, tiled=True).reshape(
        -1
    )
    column_table = (
        (arrived // size_z)[:, None] == jnp.arange(columns_xy, dtype=jnp.int32)[None, :]
    ).astype(jnp.float32)
    depth_table = (
        (arrived % size_z)[:, None] == jnp.arange(size_z, dtype=jnp.int32)[None, :]
    ).astype(jnp.float32)
    coefs = faces(padded_2(beta, (("gx", 0), ("gy", 1)), 1))
    rhs = jnp.where(live, jump_rhs, 0.0)
    start = length(rhs)
    basis = [rhs / start]
    images = []
    columns = []
    for step in range(ITERS):
        apply_vector = basis[step]
        outgoing = jnp.dot(
            spread_weight * apply_vector, slot_table, precision=lax.Precision.HIGHEST
        ).reshape(owners, capacity)
        incoming = lax.all_to_all(
            outgoing, ("gx", "gy"), split_axis=0, concat_axis=0, tiled=True
        ).reshape(-1)
        weighted = incoming[:, None] * depth_table
        apply_source = jnp.einsum(
            "sc,sz->cz", column_table, weighted, precision=lax.Precision.HIGHEST
        )
        field = chebyshev_rim(apply_source.reshape(size_x, size_y, size_z), coefs).reshape(
            columns_xy, size_z
        )
        rows_taken = jnp.dot(column_table, field, precision=lax.Precision.HIGHEST)
        picked = jnp.sum(rows_taken * depth_table, axis=1).reshape(owners, capacity)
        returned = lax.all_to_all(
            picked, ("gx", "gy"), split_axis=0, concat_axis=0, tiled=True
        ).reshape(-1)
        sampled = jnp.dot(slot_table, returned, precision=lax.Precision.HIGHEST)
        image = jnp.where(live, stiffness * apply_vector + spread_weight * sampled, 0.0)
        images.append(image)
        column = []
        remainder = image
        for vector in basis:
            height = lax.psum(jnp.sum(remainder * vector), ("gx", "gy"))
            remainder = remainder - height * vector
            column.append(height)
        norm = length(remainder)
        column.append(norm)
        columns.append(column)
        basis.append(remainder / norm)
    coeffs = least_squares(start, columns)
    solution = jnp.zeros_like(rhs)
    residual = rhs
    for step in range(ITERS):
        solution = solution + coeffs[step] * basis[step]
        residual = residual - coeffs[step] * images[step]
    return (solution, residual)


def solution(mesh):
    placed = (
        P("gx", "gy", None),
        P(("gx", "gy")),
        P(("gx", "gy")),
        P(("gx", "gy")),
        P(("gx", "gy"), None),
        P(("gx", "gy")),
        P(("gx", "gy")),
    )
    return jax.shard_map(
        on_device,
        mesh=mesh,
        in_specs=placed,
        out_specs=(P(("gx", "gy")), P(("gx", "gy"))),
        check_vma=False,
    )
```

profile of v0, /device:TPU:1, one launch (start us, length us, event | category | flops | bytes accessed | tf_op | source)
XLA Modules:
  0.0 805.1 jit_solution(16435887115055886066)
XLA Ops:
  2.6 68.7 %psum.42 = f32[]{:T(128)} all-reduce(f32[]{:T(128)} %multiply_reduce_fusion.6), channel_id=1, replica_groups=mesh['gx'=32,'gy'=4] {'gx','gy'}, use_global_device_ids=true, to_apply=%region_1.2 | all-reduce | flops 1 | bytes 8 | tf_op jit(solution)/shard_map/psum | solution.py:117
  75.6 10.6 %fusion.3 = f32[1,4096]{1,0:T(1,128)S(1)} fusion(f32[2048,1]{0,1:T(1,128)S(1)} %bitcast.75, s32[2048]{0:T(1024)S(1)} %bitcast.70), kind=kOutput, calls=%fused_computation.5 | convolution fusion | flops 109051904 | bytes 32768 | tf_op jit(solution)/shard_map/dot_general | solution.py:161
  86.9 4.7 all-to-all-start.1
  91.8 8.2 %scatter_custom_fusion = s32[4096]{0:T(1024)S(1)} fusion(s32[2048]{0:T(1024)S(1)} %broadcast_select_fusion.1, s32[2048]{0:T(1024)} %param.12, s32[]{:T(128)} %constant.72.clone.1), kind=kCustom, calls=%fused_computation.398 | custom fusion | bytes 16896
  101.4 9.1 %all-to-all-start = ((s32[128,1,32]{2,1,0:T(1,128)}), s32[128,1,32]{2,1,0:T(1,128)S(1)}, u32[]{:S(2)}, u32[]{:S(2)}) async-start(s32[128,1,32]{2,1,0:T(1,128)} %copy.10), calls=%async_computation | async-start | bytes 131072 | tf_op jit(solution)/shard_map/all_to_all | solution.py:144
  121.8 10.3 %fusion.13 = f32[1024,256]{1,0:T(8,128)S(1)} fusion(s32[4096]{0:T(1024)S(1)} %get-tuple-element.78, f32[4096]{0:T(1024)S(1)} %mul.449, s32[4096]{0:T(1024)S(1)} %get-tuple-element.77), kind=kOutput, calls=%fused_computation.15 | convolution fusion | flops 12895387648 | bytes 1097728 | tf_op jit(solution)/shard_map/sc,sz->cz/dot_general | solution.py:168
  141.8 4.0 collective-permute-start.5
  147.8 3.6 collective-permute-done.4
  167.2 3.6 collective-permute-done.8
  187.5 3.6 collective-permute-done.12
  206.3 3.6 collective-permute-done.16
  225.2 4.4 collective-permute-done.20
  239.8 8.6 %fusion.32 = f32[4096]{0:T(1024)S(1)} fusion(f32[1024,256]{1,0:T(8,128)S(1)} %bitcast.61, s32[4096]{0:T(1024)S(1)} %get-tuple-element.78, s32[4096]{0:T(1024)S(1)} %get-tuple-element.77), kind=kOutput, calls=%fused_computation.81 | convolution fusion | flops 12892237824 | bytes 1097728 | tf_op jit(solution)/shard_map/dot_general | solution.py:174
  248.5 26.6 %all_to_all.45 = f32[128,1,32]{2,1,0:T(1,128)S(1)} all-to-all(f32[128,1,32]{2,1,0:T(1,128)S(1)} %bitcast.62), channel_id=1, replica_groups=mesh['gx'=32,'gy'=4] {'gx','gy'}, dimensions={0} | all-to-all | bytes 32768 | tf_op jit(solution)/shard_map/all_to_all | solution.py:176
  276.0 14.9 %fusion.2 = f32[1,2048]{1,0:T(1,128)S(1)} fusion(f32[4096,1]{0,1:T(1,128)S(1)} %reshape.155, s32[2048]{0:T(1024)S(1)} %bitcast.71), kind=kOutput, calls=%fused_computation.4 | convolution fusion | flops 109051904 | bytes 32768 | tf_op jit(solution)/shard_map/dot_general | solution.py:179
  291.6 62.6 %psum.43 = f32[]{:T(128)} all-reduce(f32[]{:T(128)} %get-tuple-element.12), channel_id=1, replica_groups=mesh['gx'=32,'gy'=4] {'gx','gy'}, use_global_device_ids=true, to_apply=%region_8.9 | all-reduce | flops 1 | bytes 8 | tf_op jit(solution)/shard_map/psum | solution.py:185
  355.4 63.0 %psum.44 = f32[]{:T(128)} all-reduce(f32[]{:T(128)} %multiply_reduce_fusion.4), channel_id=1, replica_groups=mesh['gx'=32,'gy'=4] {'gx','gy'}, use_global_device_ids=true, to_apply=%region_10.11 | all-reduce | flops 1 | bytes 8 | tf_op jit(solution)/shard_map/psum | solution.py:117
  419.8 10.6 %fusion.1 = f32[1,4096]{1,0:T(1,128)S(1)} fusion(f32[2048,1]{0,1:T(1,128)S(1)} %bitcast.76, s32[2048]{0:T(1024)S(1)} %bitcast.72), kind=kOutput, calls=%fused_computation.3 | convolution fusion | flops 109051904 | bytes 32768 | tf_op jit(solution)/shard_map/dot_general | solution.py:161
  430.4 15.2 %all_to_all.46 = f32[128,1,32]{2,1,0:T(1,128)S(1)} all-to-all(f32[128,1,32]{2,1,0:T(1,128)S(1)} %bitcast.63), channel_id=1, replica_groups=mesh['gx'=32,'gy'=4] {'gx','gy'}, dimensions={0} | all-to-all | bytes 32768 | tf_op jit(solution)/shard_map/all_to_all | solution.py:164
  446.5 10.3 %fusion.11 = f32[1024,256]{1,0:T(8,128)S(1)} fusion(s32[4096]{0:T(1024)S(1)} %get-tuple-element.78, f32[4096]{0:T(1024)S(1)} %mul.518, s32[4096]{0:T(1024)S(1)} %get-tuple-element.77), kind=kOutput, calls=%fused_computation.14 | convolution fusion | flops 12895387648 | bytes 1097728 | tf_op jit(solution)/shard_map/sc,sz->cz/dot_general | solution.py:168
  461.7 3.6 collective-permute-done.24
  481.1 3.6 collective-permute-done.28
  500.6 3.6 collective-permute-done.32
  520.8 3.6 collective-permute-done.36
  539.7 3.6 collective-permute-done.40
  553.3 8.6 %fusion.31 = f32[4096]{0:T(1024)S(1)} fusion(f32[1024,256]{1,0:T(8,128)S(1)} %bitcast.60, s32[4096]{0:T(1024)S(1)} %get-tuple-element.78, s32[4096]{0:T(1024)S(1)} %get-tuple-element.77), kind=kOutput, calls=%fused_computation.80 | convolution fusion | flops 12892237824 | bytes 1097728 | tf_op jit(solution)/shard_map/dot_general | solution.py:174
  562.6 16.1 %all-to-all-start.4 = ((f32[128,1,32]{2,1,0:T(1,128)}), f32[128,1,32]{2,1,0:T(1,128)S(1)}, u32[]{:S(2)}, u32[]{:S(2)}) async-start(f32[128,1,32]{2,1,0:T(1,128)} %bitcast.21), calls=%async_computation.4 | async-start | bytes 131072 | tf_op jit(solution)/shard_map/all_to_all | solution.py:176
  580.6 7.9 all-to-all-done.4
  589.5 14.9 %fusion = f32[1,2048]{1,0:T(1,128)S(1)} fusion(f32[4096,1]{0,1:T(1,128)S(1)} %reshape.159, s32[2048]{0:T(1024)S(1)} %bitcast.73), kind=kOutput, calls=%fused_computation.2 | convolution fusion | flops 109051904 | bytes 32768 | tf_op jit(solution)/shard_map/dot_general | solution.py:179
  605.7 62.9 %psum.45 = f32[]{:T(128)} all-reduce(f32[]{:T(128)} %get-tuple-element.2), channel_id=1, replica_groups=mesh['gx'=32,'gy'=4] {'gx','gy'}, use_global_device_ids=true, to_apply=%region_13.14 | all-reduce | flops 1 | bytes 8 | tf_op jit(solution)/shard_map/psum | solution.py:185
  671.8 62.9 %psum.46 = f32[]{:T(128)} all-reduce(f32[]{:T(128)} %multiply_reduce_fusion.2), channel_id=1, replica_groups=mesh['gx'=32,'gy'=4] {'gx','gy'}, use_global_device_ids=true, to_apply=%region_15.16 | all-reduce | flops 1 | bytes 8 | tf_op jit(solution)/shard_map/psum | solution.py:185
  738.6 63.9 %psum.47 = f32[]{:T(128)} all-reduce(f32[]{:T(128)} %multiply_reduce_fusion.1), channel_id=1, replica_groups=mesh['gx'=32,'gy'=4] {'gx','gy'}, use_global_device_ids=true, to_apply=%region_17.18 | all-reduce | flops 1 | bytes 8 | tf_op jit(solution)/shard_map/psum | solution.py:117
  (182 shorter events, 193.5 us)
Async XLA Ops:
  86.9 14.6 %all-to-all-start.1 = ((f32[128,1,32]{2,1,0:T(1,128)}), f32[128,1,32]{2,1,0:T(1,128)S(1)}, u32[]{:S(2)}, u32[]{:S(2)}) async-start(f32[128,1,32]{2,1,0:T(1,128)} %bitcast.11), calls=%async_computation.1 | async-start | bytes 131072 | tf_op jit(solution)/shard_map/all_to_all | solution.py:164
  101.4 19.0 %all-to-all-start = ((s32[128,1,32]{2,1,0:T(1,128)}), s32[128,1,32]{2,1,0:T(1,128)S(1)}, u32[]{:S(2)}, u32[]{:S(2)}) async-start(s32[128,1,32]{2,1,0:T(1,128)} %copy.10), calls=%async_computation | async-start | bytes 131072 | tf_op jit(solution)/shard_map/all_to_all | solution.py:144
  110.5 21.9 %collective-permute-start.1 = (f32[1,64,256]{2,1,0:T(8,128)S(1)}, f32[1,64,256]{2,1,0:T(8,128)S(1)}, u32[]{:S(2)}, u32[]{:S(2)}) collective-permute-start(f32[1,64,256]{2,1,0:T(8,128)S(1)} %get-tuple-element.69), channel_id=1, source_target_pairs={{4,0},{8,4},{12,8},{16,12},{20,16},{24,20},{28,24},{32,28},{36,32}... | collective-permute-start | bytes 196616 | tf_op jit(solution)/shard_map/ppermute | solution.py:26
  113.5 18.6 %collective-permute-start = (f32[1,64,256]{2,1,0:T(8,128)S(1)}, f32[1,64,256]{2,1,0:T(8,128)S(1)}, u32[]{:S(2)}, u32[]{:S(2)}) collective-permute-start(f32[1,64,256]{2,1,0:T(8,128)S(1)} %get-tuple-element.70), channel_id=1, source_target_pairs={{0,4},{4,8},{8,12},{12,16},{16,20},{20,24},{24,28},{28,32},{32,36}... | collective-permute-start | bytes 196616 | tf_op jit(solution)/shard_map/ppermute | solution.py:25
  134.7 4.5 collective-permute-start.3
  141.8 6.0 collective-permute-start.5
  145.8 5.6 collective-permute-start.4
  153.7 4.5 collective-permute-start.6
  161.9 5.2 collective-permute-start.9
  165.2 5.6 collective-permute-start.8
  173.9 4.5 collective-permute-start.10
  182.2 5.2 collective-permute-start.13
  185.5 5.6 collective-permute-start.12
  192.8 4.5 collective-permute-start.14
  201.1 5.2 collective-permute-start.17
  204.4 5.6 collective-permute-start.16
  211.6 4.5 collective-permute-start.18
  219.9 5.2 collective-permute-start.21
  223.2 6.3 collective-permute-start.20
  457.0 4.7 collective-permute-start.25
  459.7 5.7 collective-permute-start.24
  467.6 4.5 collective-permute-start.26
  475.9 5.3 collective-permute-start.29
  479.2 5.6 collective-permute-start.28
  495.3 5.2 collective-permute-start.33
  498.6 5.6 collective-permute-start.32
  507.3 4.5 collective-permute-start.34
  515.6 5.2 collective-permute-start.37
  518.9 5.6 collective-permute-start.36
  534.4 5.2 collective-permute-start.41
  537.8 5.6 collective-permute-start.40
  562.6 26.0 %all-to-all-start.4 = ((f32[128,1,32]{2,1,0:T(1,128)}), f32[128,1,32]{2,1,0:T(1,128)S(1)}, u32[]{:S(2)}, u32[]{:S(2)}) async-start(f32[128,1,32]{2,1,0:T(1,128)} %bitcast.21), calls=%async_computation.4 | async-start | bytes 131072 | tf_op jit(solution)/shard_map/all_to_all | solution.py:176
  (23 other events, 278.3 us)
where the time goes:
time: 816 us; the launch traced here: 805 us
  blocking collectives  426 us (52%)
  starting transfers between devices  127 us (16%)
  matrix products  89.9 us (11%)
  waiting for transfers between devices  82.6 us (10%)
  other arithmetic  57.9 us (7%)
  local copies, waits for them, and re-layouts  12.4 us (2%)
  between operations  9.75 us (1%)
    psum x3, blocking collectives, length(): return jnp.sqrt(lax.psum(jnp.sum(vector * vector), ('gx', 'gy')) + EPS)  196 us
    psum x3, blocking collectives, on_device(): height = lax.psum(jnp.sum(remainder * vector), ('gx', 'gy'))  188 us
    ppermute x22, waiting for transfers between devices, padded_2(): after = lax.ppermute(leading, axis, down)  71.1 us
    ppermute x22, starting transfers between devices, padded_2(): before = lax.ppermute(last, axis, up)  59.2 us
    ppermute x22, starting transfers between devices, padded_2(): after = lax.ppermute(leading, axis, down)  37.5 us
    dot_general x2, matrix products, on_device(): sampled = jnp.dot(slot_table, returned, precision=lax.Precision.HIGHEST)  29.8 us
    add x10, other arithmetic, chebyshev_rim(): field = field + update  29.7 us
    all_to_all x1, blocking collectives, on_device(): lax.all_to_all(picked, ('gx', 'gy'), split_axis=0, concat_axis=0, tiled=T...  26.6 us
  transfers between devices with their start and end apart: 47, of which 24 were waited for; matrix products, arithmetic and copies ran while one was open for 3% of the time, Pallas kernels for 0%

commit v1 on v0

v1 whole, which is shorter than its diff:
```python
import functools

import jax
import jax.numpy as jnp
from jax import lax
from jax.experimental import pallas as pl
from jax.experimental.pallas import tpu as pltpu
from jax.sharding import PartitionSpec as P

CHEB = 6
SHIFT = 0.01
THETA = 1.025
DELTA = 0.975
SIGMA = THETA / DELTA
EPS = 1e-06
LANES = 128
PAD = 8
MESH = pl.DeviceIdType.MESH
F32 = jnp.float32
BF16 = jnp.bfloat16
CHUNK = 512


def sweep_factors():
    factors = []
    ratio = 1.0 / SIGMA
    for _ in range(CHEB - 1):
        ratio_next = 1.0 / (2.0 * SIGMA - ratio)
        factors.append((ratio_next * ratio, 2.0 * ratio_next / DELTA))
        ratio = ratio_next
    return factors


def least_squares(start, columns):
    count = len(columns)
    targets = [start] + [start * 0.0 for unused in range(count)]
    cosines = []
    sines = []
    upper = []
    for outer in range(count):
        column = list(columns[outer])
        for inner in range(outer):
            first = cosines[inner] * column[inner] + sines[inner] * column[inner + 1]
            second = -sines[inner] * column[inner] + cosines[inner] * column[inner + 1]
            column[inner] = first
            column[inner + 1] = second
        radius = jnp.sqrt(column[outer] * column[outer] + column[outer + 1] * column[outer + 1])
        cosine = column[outer] / radius
        sine = column[outer + 1] / radius
        column[outer] = radius
        targets[outer + 1] = -sine * targets[outer]
        targets[outer] = cosine * targets[outer]
        cosines.append(cosine)
        sines.append(sine)
        upper.append(column)
    coeffs = [None] * count
    for outer in reversed(range(count)):
        total = targets[outer]
        for later in range(outer + 1, count):
            total = total - upper[later][outer] * coeffs[later]
        coeffs[outer] = total / upper[outer][outer]
    return coeffs


def halves(x):
    high = x.astype(BF16)
    low = (x - high.astype(F32)).astype(BF16)
    return high, low


def nt_dot(a, b):
    return lax.dot_general(a, b, (((1,), (1,)), ((), ())), preferred_element_type=F32)


def nn_dot(a, b):
    return lax.dot_general(a, b, (((1,), (0,)), ((), ())), preferred_element_type=F32)


def total(x):
    return jnp.sum(jnp.sum(x, axis=0, keepdims=True), axis=1, keepdims=True)


def pack_row(values):
    lane = lax.broadcasted_iota(jnp.int32, (1, LANES), 1)
    row = jnp.zeros((1, LANES), F32)
    for at, value in enumerate(values):
        row = jnp.where(lane == at, value, row)
    return row


def unpack_row(row, count):
    lane = lax.broadcasted_iota(jnp.int32, (1, LANES), 1)
    return [
        jnp.sum(jnp.where(lane == at, row, 0.0), axis=1, keepdims=True) for at in range(count)
    ]


def kernel(
    n_gx,
    n_gy,
    beta,
    jump,
    stiff,
    weight,
    owner,
    cell,
    count,
    sol,
    res,
    t_one,
    l_one,
    target,
    lanes_at,
    u,
    d,
    g,
    invd,
    axl,
    axh,
    ayl,
    ayh,
    azl,
    azh,
    acc,
    field_t,
    c_one,
    z_at,
    slot_val,
    picked,
    sampled,
    y_send,
    y_recv,
    fa_send,
    fa_recv,
    fb_send,
    fb_recv,
    rb_send,
    rb_recv,
    ra_send,
    ra_recv,
    pb_send,
    pb_recv,
    pa_send,
    pa_recv,
    fa_ss,
    fa_rs,
    fb_ss,
    fb_rs,
    rb_ss,
    rb_rs,
    ra_ss,
    ra_rs,
    p_ss,
    p_rs,
    x_ss,
    x_rs,
    y_ss,
    y_rs,
):
    me_x = lax.axis_index("gx")
    me_y = lax.axis_index("gy")
    size_x, size_y, size_z = beta.shape
    rows = jump.shape[0]
    points = rows * LANES
    owners = n_gx * n_gy
    cap = LANES // n_gy
    slots = n_gx * LANES
    columns = size_x * size_y
    chunk = min(CHUNK, slots)
    lane8 = lax.broadcasted_iota(jnp.int32, (PAD, LANES), 1)

    def at_gx(shift):
        return {"gx": lax.rem(me_x + shift + n_gx, n_gx), "gy": me_y}

    def at_gy(shift):
        return {"gx": me_x, "gy": lax.rem(me_y + shift + n_gy, n_gy)}

    for p in range(2):
        for x in (0, size_x + 1):
            u[p, x] = jnp.zeros(u.shape[2:], F32)
    zero_tile = jnp.zeros((2, PAD, LANES), F32)

    def clear(x, _):
        for p in range(2):
            u[p, x, :, 0:PAD, :] = zero_tile
            u[p, x, :, PAD + size_y : 2 * PAD + size_y, :] = zero_tile
        return 0

    lax.fori_loop(1, size_x + 1, clear, 0)

    barrier = pltpu.get_barrier_semaphore()

    def greet_x(k, _):
        pl.semaphore_signal(barrier, inc=1, device_id=at_gx(k), device_id_type=MESH)
        return 0

    def greet_y(k, _):
        pl.semaphore_signal(barrier, inc=1, device_id=at_gy(k), device_id_type=MESH)
        return 0

    lax.fori_loop(1, n_gx, greet_x, 0)
    lax.fori_loop(1, n_gy, greet_y, 0)

    def gx_copy(src, dst, send, recv, k, sign):
        return pltpu.make_async_remote_copy(
            src_ref=src,
            dst_ref=dst,
            send_sem=send,
            recv_sem=recv,
            device_id=at_gx(sign * k),
            device_id_type=MESH,
        )

    def gy_copy(src, dst, send, recv, k, sign):
        return pltpu.make_async_remote_copy(
            src_ref=src,
            dst_ref=dst,
            send_sem=send,
            recv_sem=recv,
            device_id=at_gy(sign * k),
            device_id_type=MESH,
        )

    def wait_for(ref, sem):
        pltpu.make_async_copy(ref, ref, sem).wait()

    def send_gx(src, dst, send, recv, sign):
        def body(k, _):
            gx_copy(src.at[k], dst.at[k], send, recv, k, sign).start()
            return 0

        lax.fori_loop(1, n_gx, body, 0)

    def halo_copies(p, which):
        rows_in = pl.ds(PAD, size_y)
        copies = (
            (
                me_x > 0,
                lambda: gx_copy(
                    u.at[p, 1, :, rows_in, :],
                    u.at[p, size_x + 1, :, rows_in, :],
                    x_ss.at[p, 0],
                    x_rs.at[p, 1],
                    1,
                    -1,
                ),
            ),
            (
                me_x < n_gx - 1,
                lambda: gx_copy(
                    u.at[p, size_x, :, rows_in, :],
                    u.at[p, 0, :, rows_in, :],
                    x_ss.at[p, 1],
                    x_rs.at[p, 0],
                    1,
                    1,
                ),
            ),
            (
                me_y > 0,
                lambda: gy_copy(
                    y_send.at[p, 0], y_recv.at[p, 1], y_ss.at[p, 0], y_rs.at[p, 1], 1, -1
                ),
            ),
            (
                me_y < n_gy - 1,
                lambda: gy_copy(
                    y_send.at[p, 1], y_recv.at[p, 0], y_ss.at[p, 1], y_rs.at[p, 0], 1, 1
                ),
            ),
        )
        return [copies[i] for i in which]

    def halo_send_x(p):
        for on, copy in halo_copies(p, (0, 1)):
            pl.when(on)(lambda: copy().start())

    def halo_send_y(p):
        def pack(x, _):
            for h in range(2):
                y_send[p, 0, x, h] = u[p, x + 1, h, PAD : PAD + 1, :]
                y_send[p, 1, x, h] = u[p, x + 1, h, PAD + size_y - 1 : PAD + size_y, :]
            return 0

        lax.fori_loop(0, size_x, pack, 0)
        for on, copy in halo_copies(p, (2, 3)):
            pl.when(on)(lambda: copy().start())

    def halo_wait_sent(p):
        for on, copy in halo_copies(p, range(4)):
            pl.when(on)(lambda: copy().wait_send())

    def halo_wait(p):
        (_, down_x), (_, up_x), (_, down_y), (_, up_y) = halo_copies(p, range(4))
        pl.when(me_x < n_gx - 1)(lambda: down_x().wait_recv())
        pl.when(me_x > 0)(lambda: up_x().wait_recv())

        @pl.when(me_y < n_gy - 1)
        def _():
            down_y().wait_recv()

            def unpack(x, _):
                for h in range(2):
                    u[p, x + 1, h, PAD + size_y : PAD + size_y + 1, :] = y_recv[p, 1, x, h]
                return 0

            lax.fori_loop(0, size_x, unpack, 0)

        @pl.when(me_y > 0)
        def _():
            up_y().wait_recv()

            def unpack(x, _):
                for h in range(2):
                    u[p, x + 1, h, PAD - 1 : PAD, :] = y_recv[p, 0, x, h]
                return 0

            lax.fori_loop(0, size_x, unpack, 0)

    shift_gy = n_gy.bit_length() - 1
    own = owner[...]
    target[...] = ((own & (n_gy - 1)) - me_y & (n_gy - 1)) * n_gx + (
        (own >> shift_gy) - me_x & (n_gx - 1)
    )
    iota_t = lax.broadcasted_iota(jnp.int32, (owners, LANES), 0)
    iota_l = lax.broadcasted_iota(jnp.int32, (LANES, LANES), 0)
    above = lax.broadcasted_iota(jnp.int32, (LANES, 2 * LANES), 1)
    below = lax.broadcasted_iota(jnp.int32, (LANES, 2 * LANES), 0)
    counter = ((below < above) | (above >= LANES)).astype(BF16)
    offset = jnp.zeros((owners, LANES), F32)
    for j in range(rows):
        hit = target[j : j + 1, :] == iota_t
        hit_f = jnp.where(hit, 1.0, 0.0)
        hit_b = hit_f.astype(BF16)
        t_one[:, j * LANES : (j + 1) * LANES] = hit_b
        both = nn_dot(hit_b, counter)
        rank = jnp.sum(hit_f * (both[:, :LANES] + offset), axis=0, keepdims=True)
        offset = offset + both[:, LANES:]
        lane_of = rank.astype(jnp.int32) + me_y * cap
        l_one[:, j * LANES : (j + 1) * LANES] = jnp.where(lane_of == iota_l, 1.0, 0.0).astype(BF16)

    def to_rows(vector, row_of):
        out = jnp.zeros((owners, LANES), F32)
        for j in range(rows):
            cols = slice(j * LANES, (j + 1) * LANES)
            for part in row_of(vector[j : j + 1, :]):
                spread = t_one[:, cols] * part
                out = out + nt_dot(spread, l_one[:, cols])
        return out

    def split_index(row):
        low = (row & (2 * LANES - 1)) + 1
        middle = (row >> 8) & (2 * LANES - 1)
        high = row >> 16
        return [
            x.astype(F32).astype(BF16) for x in (low, middle * 256, high * 65536)
        ]

    def forward_a(f, first, second):
        for k in range(n_gy):
            fa_send[f, k, 0:n_gx, :] = first[k * n_gx : (k + 1) * n_gx, :]
            fa_send[f, k, n_gx : 2 * n_gx, :] = second[k]
        for k in range(1, n_gy):
            gy_copy(fa_send.at[f, k], fa_recv.at[f, k], fa_ss.at[f], fa_rs.at[f], k, 1).start()

    def forward_b(f):
        wait_for(fa_recv.at[f, pl.ds(1, n_gy - 1)], fa_rs.at[f])
        both = fa_send[f, 0]
        for k in range(1, n_gy):
            both = both + fa_recv[f, k]
        for k in range(n_gx):
            fb_send[f, k, 0:1, :] = both[k : k + 1, :]
            fb_send[f, k, 1:2, :] = both[n_gx + k : n_gx + k + 1, :]
        send_gx(fb_send.at[f], fb_recv.at[f], fb_ss.at[f], fb_rs.at[f], 1)
        fb_recv[f, 0] = fb_send[f, 0]

    def forward_c(f):
        wait_for(fb_recv.at[f, pl.ds(1, n_gx - 1)], fb_rs.at[f])
        return fb_recv[f, :, 0, :], fb_recv[f, :, 1, :]

    def back_a(f, second):
        for k in range(n_gx):
            rb_send[f, k, 0:1, :] = picked[k : k + 1, :]
            rb_send[f, k, 1:2, :] = second
        send_gx(rb_send.at[f], rb_recv.at[f], rb_ss.at[f], rb_rs.at[f], -1)
        rb_recv[f, 0] = rb_send[f, 0]

    def back_b(f):
        wait_for(rb_recv.at[f, pl.ds(1, n_gx - 1)], rb_rs.at[f])
        ra_send[f, 0:n_gx, :] = rb_recv[f, :, 0, :]
        ra_send[f, n_gx : 2 * n_gx, :] = rb_recv[f, :, 1, :]
        for k in range(1, n_gy):
            gy_copy(ra_send.at[f], ra_recv.at[f, k], ra_ss.at[f], ra_rs.at[f], k, -1).start()

    def back_c(f):
        wait_for(ra_recv.at[f, pl.ds(1, n_gy - 1)], ra_rs.at[f])
        blocks = [ra_send[f]] + [ra_recv[f, k] for k in range(1, n_gy)]
        high, low = halves(jnp.concatenate([b[0:n_gx, :] for b in blocks], axis=0))
        rest = blocks[0][n_gx:, :]
        for b in blocks[1:]:
            rest = rest + b[n_gx:, :]
        for j in range(rows):
            cols = slice(j * LANES, (j + 1) * LANES)
            lanes = l_one[:, cols]
            found = nn_dot(high, lanes) + nn_dot(low, lanes)
            sampled[j : j + 1, :] = jnp.sum(
                found * t_one[:, cols].astype(F32), axis=0, keepdims=True
            )
        return sampled[...], jnp.sum(rest, axis=0, keepdims=True)

    live = lax.broadcasted_iota(jnp.int32, (rows, LANES), 0) < count[...]
    rhs = jnp.where(live, jump[...], 0.0)
    sw = weight[...]
    cells = cell[...]
    index_rows = to_rows(cells, split_index)
    value_rows = to_rows(sw * rhs, halves)
    pl.semaphore_wait(barrier, n_gx + n_gy - 2)
    forward_a(0, index_rows, [value_rows[k * n_gx : (k + 1) * n_gx, :] for k in range(n_gy)])

    def place(x, _):
        for h in range(2):
            u[1, x + 1, h, PAD : PAD + size_y, :] = beta[x, :, h * LANES : (h + 1) * LANES]
        return 0

    lax.fori_loop(0, size_x, place, 0)
    halo_send_x(1)
    halo_send_y(1)
    forward_b(0)

    def rows_at(ref, p, x, h, start, n):
        return ref[p, x, h, pl.ds(start, n), :]

    def z_sides(low, high, lane):
        low_up, high_up = pltpu.roll(low, 1, 1), pltpu.roll(high, 1, 1)
        low_dn, high_dn = pltpu.roll(low, LANES - 1, 1), pltpu.roll(high, LANES - 1, 1)
        return (
            (low_up, jnp.where(lane == 0, low_up, high_up)),
            (jnp.where(lane == LANES - 1, high_dn, low_dn), high_dn),
        )

    def harmonic(a, b):
        return 2.0 * a * b / (a + b)

    halo_wait(1)

    def coefficients(step, _):
        x = step // (size_y // PAD)
        y = (step % (size_y // PAD)) * PAD
        centre = [rows_at(u, 1, x + 1, h, y + PAD, PAD) for h in range(2)]
        before, after = z_sides(centre[0], centre[1], lane8)
        for h in range(2):
            c = centre[h]
            kxl = harmonic(c, rows_at(u, 1, x, h, y + PAD, PAD))
            kxh = harmonic(c, rows_at(u, 1, x + 2, h, y + PAD, PAD))
            kyl = harmonic(c, rows_at(u, 1, x + 1, h, y + PAD - 1, PAD))
            kyh = harmonic(c, rows_at(u, 1, x + 1, h, y + PAD + 1, PAD))
            kzl = harmonic(c, before[h])
            kzh = harmonic(c, after[h])
            if h == 0:
                kzl = jnp.where(lane8 == 0, 0.0, kzl)
            else:
                kzh = jnp.where(lane8 == LANES - 1, 0.0, kzh)
            inverse = 1.0 / (SHIFT + kxl + kxh + kyl + kyh + kzl + kzh)
            at = (x, h, pl.ds(y, PAD), slice(None))
            invd[at] = inverse
            axl[at] = kxl * inverse
            axh[at] = kxh * inverse
            ayl[at] = kyl * inverse
            ayh[at] = kyh * inverse
            azl[at] = kzl * inverse
            azh[at] = kzh * inverse
        return 0

    lax.fori_loop(0, size_x * (size_y // PAD), coefficients, 0)
    halo_wait_sent(1)

    index, values = forward_c(0)
    index = index.astype(jnp.int32) - 1
    z_at[...] = jnp.where(index < 0, -1, index & (size_z - 1))
    slot_val[...] = index >> 8
    iota_c = lax.broadcasted_iota(jnp.int32, (columns, LANES), 0)
    per = chunk // LANES

    def column_table(j, _):
        row = slot_val[pl.ds(j, 1), :]
        c_one[j] = jnp.where(row == iota_c, 1.0, 0.0).astype(BF16)
        return 0

    lax.fori_loop(0, n_gx, column_table, 0)
    iota_z = lax.broadcasted_iota(jnp.int32, (size_z, LANES), 0)

    def spread_grid(values):
        picked[...] = values
        acc[...] = jnp.zeros_like(acc)

        def body(i, _):
            high_parts, low_parts, col_parts = [], [], []
            for q in range(per):
                j = i * per + q
                row = picked[pl.ds(j, 1), :]
                hit = z_at[pl.ds(j, 1), :] == iota_z
                high = row.astype(BF16).astype(F32)
                high_parts.append(jnp.where(hit, high, 0.0).astype(BF16))
                low_parts.append(jnp.where(hit, row - high, 0.0).astype(BF16))
                col_parts.append(c_one[j])
            cols = jnp.concatenate(col_parts, axis=1)
            acc[...] += nt_dot(cols, jnp.concatenate(high_parts, axis=1)) + nt_dot(
                cols, jnp.concatenate(low_parts, axis=1)
            )
            return 0

        lax.fori_loop(0, slots // chunk, body, 0)

    def sample_grid(p):
        def turn(x, _):
            for h in range(2):
                high, low = halves(u[p, x + 1, h, PAD : PAD + size_y, :].T)
                field_t[x, h * LANES : (h + 1) * LANES, :] = high
                field_t[x, size_z + h * LANES : size_z + (h + 1) * LANES, :] = low
            return 0

        lax.fori_loop(0, size_x, turn, 0)
        whole = jnp.concatenate([field_t[x] for x in range(size_x)], axis=1)

        def body(i, _):
            found = nn_dot(
                whole, jnp.concatenate([c_one[i * per + q] for q in range(per)], axis=1)
            )
            for q in range(per):
                j = i * per + q
                hit = z_at[pl.ds(j, 1), :] == iota_z
                cols = slice(q * LANES, (q + 1) * LANES)
                both = found[:size_z, cols] + found[size_z:, cols]
                picked[pl.ds(j, 1), :] = jnp.sum(
                    jnp.where(hit, both, 0.0), axis=0, keepdims=True
                )
            return 0

        lax.fori_loop(0, slots // chunk, body, 0)

    def relax(p, x, y, n, first, second):
        lane = lax.broadcasted_iota(jnp.int32, (n, LANES), 1)
        centre = [rows_at(u, p, x + 1, h, y + PAD, n) for h in range(2)]
        before, after = z_sides(centre[0], centre[1], lane)
        for h in range(2):
            at = (x, h, pl.ds(y, n), slice(None))
            image = g[at] - centre[h]
            image += axl[at] * rows_at(u, p, x, h, y + PAD, n)
            image += axh[at] * rows_at(u, p, x + 2, h, y + PAD, n)
            image += ayl[at] * rows_at(u, p, x + 1, h, y + PAD - 1, n)
            image += ayh[at] * rows_at(u, p, x + 1, h, y + PAD + 1, n)
            image += azl[at] * before[h] + azh[at] * after[h]
            update = first * d[at] + second * image
            d[at] = update
            u[1 - p, x + 1, h, pl.ds(y + PAD, n), :] = centre[h] + update

    tiles = size_y // PAD

    def pressure():
        def begin(x, _):
            for h in range(2):
                source = acc[pl.ds(x * size_y, size_y), h * LANES : (h + 1) * LANES]
                scaled = source * invd[x, h]
                g[x, h] = scaled
                scaled = scaled * (1.0 / THETA)
                d[x, h] = scaled
                u[0, x + 1, h, PAD : PAD + size_y, :] = scaled
            return 0

        lax.fori_loop(0, size_x, begin, 0)
        halo_send_x(0)
        halo_send_y(0)
        for step, (first, second) in enumerate(sweep_factors()):
            p = step % 2
            last = step == CHEB - 2
            halo_wait(p)
            if step > 0:
                halo_wait_sent(1 - p)

            def side(i, _):
                x = lax.rem(i, 2) * (size_x - 1)
                relax(p, x, (i // 2) * PAD, PAD, first, second)
                return 0

            lax.fori_loop(0, 2 * tiles, side, 0)
            if not last:
                halo_send_x(1 - p)

            def edge(x, _):
                relax(p, x, 0 * x, PAD, first, second)
                relax(p, x, 0 * x + (size_y - PAD), PAD, first, second)
                return 0

            lax.fori_loop(1, size_x - 1, edge, 0)
            if not last:
                halo_send_y(1 - p)

            def inner(i, _):
                x = 1 + i // (tiles - 2)
                y = (1 + lax.rem(i, tiles - 2)) * PAD
                relax(p, x, y, PAD, first, second)
                return 0

            lax.fori_loop(0, (size_x - 2) * (tiles - 2), inner, 0)
        halo_wait_sent((CHEB - 2) % 2)
        return (CHEB - 1) % 2

    zero_row = jnp.zeros((1, LANES), F32)
    spread_grid(values)
    sample_grid(pressure())
    back_a(0, zero_row)
    back_b(0)
    got, _ = back_c(0)
    steady = stiff[...]
    image_1 = jnp.where(live, steady * rhs + sw * got, 0.0)

    partial = pack_row([total(rhs * rhs), total(rhs * image_1), total(image_1 * image_1)])
    partial_rows = jnp.broadcast_to(partial, (n_gx, LANES))
    forward_a(1, to_rows(sw * image_1, halves), [partial_rows] * n_gy)
    forward_b(1)
    values, sums = forward_c(1)
    sum_bb, sum_ab, _ = unpack_row(jnp.sum(sums, axis=0, keepdims=True), 3)
    start = jnp.sqrt(sum_bb + EPS)
    scale = 1.0 / start
    v_1 = rhs * scale
    w_1 = image_1 * scale
    h_11 = sum_ab * scale * scale
    rest_1 = w_1 - h_11 * v_1
    spread_grid(values)
    sample_grid(pressure())
    back_a(1, pack_row([total(rest_1 * rest_1)]))
    back_b(1)
    got, sums = back_c(1)
    image_2 = jnp.where(live, steady * image_1 + sw * got, 0.0)
    h_21 = jnp.sqrt(unpack_row(sums, 1)[0] + EPS)
    v_2 = rest_1 / h_21
    w_2 = (image_2 * scale - h_11 * w_1) / h_21

    partial = pack_row(
        [total(w_2 * v_1), total(w_2 * v_2), total(w_2 * w_2), total(v_1 * v_1), total(v_1 * v_2),
         total(v_2 * v_2)]
    )
    pb_send[...] = jnp.broadcast_to(partial, pb_send.shape)

    def spill(k, _):
        gx_copy(pb_send, pb_recv.at[k], p_ss.at[0], p_rs.at[0], k, 1).start()
        return 0

    lax.fori_loop(1, n_gx, spill, 0)
    pb_recv[0] = pb_send[...]
    wait_for(pb_recv.at[pl.ds(1, n_gx - 1)], p_rs.at[0])
    pa_send[...] = jnp.sum(pb_recv[...], axis=0)
    for k in range(1, n_gy):
        gy_copy(pa_send, pa_recv.at[k], p_ss.at[1], p_rs.at[1], k, 1).start()
    pa_recv[0] = pa_send[...]
    wait_for(pa_recv.at[pl.ds(1, n_gy - 1)], p_rs.at[1])
    sums = jnp.sum(pa_recv[...], axis=0)[0:1, :]
    w2v1, w2v2, w2w2, v1v1, v1v2, v2v2 = unpack_row(sums, 6)
    h_12 = w2v1
    h_22 = w2v2 - h_12 * v1v2
    square = (
        w2w2
        + h_12 * h_12 * v1v1
        + h_22 * h_22 * v2v2
        - 2.0 * h_12 * w2v1
        - 2.0 * h_22 * w2v2
        + 2.0 * h_12 * h_22 * v1v2
    )
    h_32 = jnp.sqrt(jnp.maximum(square, 0.0) + EPS)
    y_1, y_2 = least_squares(start, [[h_11, h_21], [h_12, h_22, h_32]])
    sol[...] = y_1 * v_1 + y_2 * v_2
    res[...] = rhs - y_1 * w_1 - y_2 * w_2

    for f in range(2):
        for k in range(1, n_gy):
            gy_copy(fa_send.at[f, k], fa_recv.at[f, k], fa_ss.at[f], fa_rs.at[f], k, 1).wait_send()
            gy_copy(ra_send.at[f], ra_recv.at[f, k], ra_ss.at[f], ra_rs.at[f], k, -1).wait_send()
        wait_for(fb_send.at[f, pl.ds(1, n_gx - 1)], fb_ss.at[f])
        wait_for(rb_send.at[f, pl.ds(1, n_gx - 1)], rb_ss.at[f])
    wait_for(pb_recv.at[pl.ds(1, n_gx - 1)], p_ss.at[0])
    wait_for(pa_recv.at[pl.ds(1, n_gy - 1)], p_ss.at[1])


def on_device(n_gx, n_gy, beta, jump, stiff, weight, owner, cell, count):
    size_x, size_y, size_z = beta.shape
    points = jump.shape[0]
    rows = points // LANES
    owners = n_gx * n_gy
    columns = size_x * size_y
    tile = (size_x, 2, size_y, LANES)
    dma = pltpu.SemaphoreType.DMA
    scratch = [
        pltpu.VMEM((owners, points), BF16),
        pltpu.VMEM((LANES, points), BF16),
        pltpu.VMEM((rows, LANES), jnp.int32),
        pltpu.VMEM((rows, LANES), jnp.int32),
        pltpu.VMEM((2, size_x + 2, 2, size_y + 2 * PAD, LANES), F32),
        pltpu.VMEM(tile, F32),
        pltpu.VMEM(tile, F32),
        pltpu.VMEM(tile, F32),
        pltpu.VMEM(tile, F32),
        pltpu.VMEM(tile, F32),
        pltpu.VMEM(tile, F32),
        pltpu.VMEM(tile, F32),
        pltpu.VMEM(tile, F32),
        pltpu.VMEM(tile, F32),
        pltpu.VMEM((columns, size_z), F32),
        pltpu.VMEM((size_x, 2 * size_z, size_y), BF16),
        pltpu.VMEM((n_gx, columns, LANES), BF16),
        pltpu.VMEM((n_gx, LANES), jnp.int32),
        pltpu.VMEM((n_gx, LANES), jnp.int32),
        pltpu.VMEM((n_gx, LANES), F32),
        pltpu.VMEM((rows, LANES), F32),
        pltpu.VMEM((2, 2, size_x, 2, 1, LANES), F32),
        pltpu.VMEM((2, 2, size_x, 2, 1, LANES), F32),
        pltpu.VMEM((2, n_gy, 2 * n_gx, LANES), F32),
        pltpu.VMEM((2, n_gy, 2 * n_gx, LANES), F32),
        pltpu.VMEM((2, n_gx, 2, LANES), F32),
        pltpu.VMEM((2, n_gx, 2, LANES), F32),
        pltpu.VMEM((2, n_gx, 2, LANES), F32),
        pltpu.VMEM((2, n_gx, 2, LANES), F32),
        pltpu.VMEM((2, 2 * n_gx, LANES), F32),
        pltpu.VMEM((2, n_gy, 2 * n_gx, LANES), F32),
        pltpu.VMEM((2, LANES), F32),
        pltpu.VMEM((n_gx, 2, LANES), F32),
        pltpu.VMEM((2, LANES), F32),
        pltpu.VMEM((n_gy, 2, LANES), F32),
    ] + [dma((2,))] * 10 + [dma((2, 2))] * 4
    vmem = pl.BlockSpec(memory_space=pltpu.VMEM)
    out = jax.ShapeDtypeStruct((rows, LANES), F32)
    solution, residual = pl.pallas_call(
        functools.partial(kernel, n_gx, n_gy),
        out_shape=(out, out),
        in_specs=[vmem] * 7,
        out_specs=(vmem, vmem),
        scratch_shapes=scratch,
        compiler_params=pltpu.CompilerParams(
            collective_id=0, has_side_effects=True, vmem_limit_bytes=56 * 1024 * 1024
        ),
    )(
        beta,
        jump.reshape(rows, LANES),
        stiff.reshape(rows, LANES),
        weight.reshape(rows, LANES),
        owner.reshape(rows, LANES),
        cell.reshape(rows, LANES),
        count.reshape(1, 1),
    )
    return solution.reshape(points), residual.reshape(points)


def solution(mesh):
    points = P(("gx", "gy"))
    return jax.shard_map(
        functools.partial(on_device, mesh.shape["gx"], mesh.shape["gy"]),
        mesh=mesh,
        in_specs=(P("gx", "gy", None), points, points, points, P(("gx", "gy"), None), points, points),
        out_specs=(points, points),
        check_vma=False,
    )
```

time: 816 us -> 197 us (0.24); the launches traced: 805 us -> 197 us
  blocking collectives: 426 us -> 0 us
  Pallas kernels: 0 us -> 193 us
  starting transfers between devices: 127 us -> 0 us
  matrix products: 89.9 us -> 0 us
  waiting for transfers between devices: 82.6 us -> 0 us
  other arithmetic: 57.9 us -> 0 us
  local copies, waits for them, and re-layouts: 12.4 us -> 1.9 us
  between operations: 9.75 us -> 1.3 us
    psum x6 -> x0, blocking collectives: 384 us -> none  [the longest x3 196 us: length(): return jnp.sqrt(lax.psum(jnp.sum(vector * vector), ('gx', 'gy')) + EPS)]
    pallas_call x0 -> x1, Pallas kernels: none -> 193 us  [on_device(): pl.pallas_call(functools.partial(kernel, n_gx, n_gy), out_shape=(out, out...]
    ppermute x44 -> x0, starting transfers between devices: 96.8 us -> none  [the longest x22 59.2 us: padded_2(): before = lax.ppermute(last, axis, up)]
    dot_general x9 -> x0, matrix products: 89.9 us -> none  [the longest x2 29.8 us: on_device(): sampled = jnp.dot(slot_table, returned, precision=lax.Precision.HIGHEST)]
    ppermute x44 -> x0, waiting for transfers between devices: 71.1 us -> none  [the longest x22 71.1 us: padded_2(): after = lax.ppermute(leading, axis, down)]
    all_to_all x2 -> x0, blocking collectives: 41.8 us -> none  [the longest x1 26.6 us: on_device(): lax.all_to_all(picked, ('gx', 'gy'), split_axis=0, concat_axis=0, tiled=T...]
    add x11 -> x0, other arithmetic: 30.4 us -> none  [the longest x10 29.7 us: chebyshev_rim(): field = field + update]
    all_to_all x3 -> x0, starting transfers between devices: 29.8 us -> none  [the longest x1 16.1 us: on_device(): lax.all_to_all(picked, ('gx', 'gy'), split_axis=0, concat_axis=0, tiled=T...]
  transfers between devices with their start and end apart: 47 -> 0, of which waited for: 24 -> 0; matrix products, arithmetic and copies ran while one was open for 3% -> 0% of each run, Pallas kernels for 0% -> 0%
where the time goes in v1:
time: 197 us
  Pallas kernels  193 us (98%)
    pallas_call x1, Pallas kernels, on_device(): pl.pallas_call(functools.partial(kernel, n_gx, n_gy), out_shape=(out, out...  193 us

profile of v1, /device:TPU:1, one launch (start us, length us, event | category | flops | bytes accessed | tf_op | source)
XLA Modules:
  0.0 196.6 jit_solution(15656911446006533604)
XLA Ops:
  1.3 193.4 %shard_map.86 = (f32[16,128]{1,0:T(8,128)}, f32[16,128]{1,0:T(8,128)}) custom-call(f32[16,64,256]{2,1,0:T(8,128)} %beta.1, f32[16,128]{1,0:T(8,128)} %bitcast.9, f32[16,128]{1,0:T(8,128)} %bitcast.10, f32[16,128]{1,0:T(8,128)} %bitcast.11, s32[16,128]{1,0:T(8,128)} %bitcast.12, s32[16,128]{1,0:T(8,128)} %bitcast.13, s32[1,1]{1,0:T(1,128)} %bitcast.8.count), custom_call_target="tpu_custom_call" | custom-call | tf_op jit(solution)/shard_map/pallas_call | solution.py:731
  194.7 0.0 copy-start
  194.7 1.3 copy.12
  196.0 0.0 copy-done
  196.0 0.6 copy.13
Async XLA Ops:
  194.7 1.3 copy-start

commit v2 on v1

--- a/solution.py
+++ b/solution.py
@@ -443,9 +443,7 @@
 
     halo_wait(1)
 
-    def coefficients(step, _):
-        x = step // (size_y // PAD)
-        y = (step % (size_y // PAD)) * PAD
+    def coefficients(x, y):
         centre = [rows_at(u, 1, x + 1, h, y + PAD, PAD) for h in range(2)]
         before, after = z_sides(centre[0], centre[1], lane8)
         for h in range(2):
@@ -469,9 +467,14 @@
             ayh[at] = kyh * inverse
             azl[at] = kzl * inverse
             azh[at] = kzh * inverse
+
+    def coefficient_planes(i, _):
+        for x in range(2):
+            for y in range(0, size_y, PAD):
+                coefficients(2 * i + x, y)
         return 0
 
-    lax.fori_loop(0, size_x * (size_y // PAD), coefficients, 0)
+    lax.fori_loop(0, size_x // 2, coefficient_planes, 0)
     halo_wait_sent(1)
 
     index, values = forward_c(0)
@@ -554,8 +557,6 @@
             d[at] = update
             u[1 - p, x + 1, h, pl.ds(y + PAD, n), :] = centre[h] + update
 
-    tiles = size_y // PAD
-
     def pressure():
         def begin(x, _):
             for h in range(2):
@@ -577,31 +578,20 @@
             if step > 0:
                 halo_wait_sent(1 - p)
 
-            def side(i, _):
-                x = lax.rem(i, 2) * (size_x - 1)
-                relax(p, x, (i // 2) * PAD, PAD, first, second)
-                return 0
-
-            lax.fori_loop(0, 2 * tiles, side, 0)
+            for x in (0, size_x - 1):
+                for y in range(0, size_y, 2 * PAD):
+                    relax(p, x, y, 2 * PAD, first, second)
             if not last:
                 halo_send_x(1 - p)
-
-            def edge(x, _):
-                relax(p, x, 0 * x, PAD, first, second)
-                relax(p, x, 0 * x + (size_y - PAD), PAD, first, second)
-                return 0
-
-            lax.fori_loop(1, size_x - 1, edge, 0)
+            middle = range(1, size_x - 1)
+            for x in middle:
+                relax(p, x, 0, PAD, first, second)
+                relax(p, x, size_y - PAD, PAD, first, second)
             if not last:
                 halo_send_y(1 - p)
-
-            def inner(i, _):
-                x = 1 + i // (tiles - 2)
-                y = (1 + lax.rem(i, tiles - 2)) * PAD
-                relax(p, x, y, PAD, first, second)
-                return 0
-
-            lax.fori_loop(0, (size_x - 2) * (tiles - 2), inner, 0)
+            for x in middle:
+                for y in range(PAD, size_y - PAD, 2 * PAD):
+                    relax(p, x, y, 2 * PAD, first, second)
         halo_wait_sent((CHEB - 2) % 2)
         return (CHEB - 1) % 2
 

time: 197 us -> 131 us (0.66)
  Pallas kernels: 193 us -> 128 us
    pallas_call x1, Pallas kernels: 193 us -> 128 us  [on_device(): pl.pallas_call(functools.partial(kernel, n_gx, n_gy), out_shape=(out, out...]
where the time goes in v2:
time: 131 us
  Pallas kernels  128 us (98%)
  local copies, waits for them, and re-layouts  1.9 us (1%)
    pallas_call x1, Pallas kernels, on_device(): pl.pallas_call(functools.partial(kernel, n_gx, n_gy), out_shape=(out, out...  128 us

profile of v2, /device:TPU:1, one launch (start us, length us, event | category | flops | bytes accessed | tf_op | source)
XLA Modules:
  0.0 131.2 jit_solution(954773058209750630)
XLA Ops:
  1.3 128.0 %shard_map.86 = (f32[16,128]{1,0:T(8,128)}, f32[16,128]{1,0:T(8,128)}) custom-call(f32[16,64,256]{2,1,0:T(8,128)} %beta.1, f32[16,128]{1,0:T(8,128)} %bitcast.9, f32[16,128]{1,0:T(8,128)} %bitcast.10, f32[16,128]{1,0:T(8,128)} %bitcast.11, s32[16,128]{1,0:T(8,128)} %bitcast.12, s32[16,128]{1,0:T(8,128)} %bitcast.13, s32[1,1]{1,0:T(1,128)} %bitcast.8.count), custom_call_target="tpu_custom_call" | custom-call | tf_op jit(solution)/shard_map/pallas_call | solution.py:721
  129.3 0.0 copy-start
  129.3 1.3 copy.12
  130.6 0.0 copy-done
  130.6 0.6 copy.13
Async XLA Ops:
  129.3 1.3 %copy-start = (f32[16,128]{1,0:T(8,128)S(1)}, f32[16,128]{1,0:T(8,128)}, u32[]{:S(2)}) copy-start(f32[16,128]{1,0:T(8,128)} %get-tuple-element.5) | copy-start | bytes 24580

commit v3 on v2

v3 whole, which is shorter than its diff:
```python
import functools

import jax
import jax.numpy as jnp
from jax import lax
from jax.experimental import pallas as pl
from jax.experimental.pallas import tpu as pltpu
from jax.sharding import PartitionSpec as P

CHEB = 6
SHIFT = 0.01
THETA = 1.025
DELTA = 0.975
SIGMA = THETA / DELTA
EPS = 1e-06
LANES = 128
PAD = 8
EDGE = 2 * PAD
PARTS = 2
DEPTH = CHEB - 1
SIDES = [(x, y) for x in (-1, 0, 1) for y in (-1, 0, 1) if (x, y) != (0, 0)]
MESH = pl.DeviceIdType.MESH
F32 = jnp.float32
BF16 = jnp.bfloat16
CHUNK = 512


def sweep_factors():
    factors = []
    ratio = 1.0 / SIGMA
    for _ in range(CHEB - 1):
        ratio_next = 1.0 / (2.0 * SIGMA - ratio)
        factors.append((ratio_next * ratio, 2.0 * ratio_next / DELTA))
        ratio = ratio_next
    return factors


def least_squares(start, columns):
    count = len(columns)
    targets = [start] + [start * 0.0 for unused in range(count)]
    cosines = []
    sines = []
    upper = []
    for outer in range(count):
        column = list(columns[outer])
        for inner in range(outer):
            first = cosines[inner] * column[inner] + sines[inner] * column[inner + 1]
            second = -sines[inner] * column[inner] + cosines[inner] * column[inner + 1]
            column[inner] = first
            column[inner + 1] = second
        radius = jnp.sqrt(column[outer] * column[outer] + column[outer + 1] * column[outer + 1])
        cosine = column[outer] / radius
        sine = column[outer + 1] / radius
        column[outer] = radius
        targets[outer + 1] = -sine * targets[outer]
        targets[outer] = cosine * targets[outer]
        cosines.append(cosine)
        sines.append(sine)
        upper.append(column)
    coeffs = [None] * count
    for outer in reversed(range(count)):
        total = targets[outer]
        for later in range(outer + 1, count):
            total = total - upper[later][outer] * coeffs[later]
        coeffs[outer] = total / upper[outer][outer]
    return coeffs


def halves(x):
    high = x.astype(BF16)
    low = (x - high.astype(F32)).astype(BF16)
    return high, low


def nt_dot(a, b):
    return lax.dot_general(a, b, (((1,), (1,)), ((), ())), preferred_element_type=F32)


def nn_dot(a, b):
    return lax.dot_general(a, b, (((1,), (0,)), ((), ())), preferred_element_type=F32)


def total(x):
    return jnp.sum(jnp.sum(x, axis=0, keepdims=True), axis=1, keepdims=True)


def pack_row(values):
    lane = lax.broadcasted_iota(jnp.int32, (1, LANES), 1)
    row = jnp.zeros((1, LANES), F32)
    for at, value in enumerate(values):
        row = jnp.where(lane == at, value, row)
    return row


def unpack_row(row, count):
    lane = lax.broadcasted_iota(jnp.int32, (1, LANES), 1)
    return [
        jnp.sum(jnp.where(lane == at, row, 0.0), axis=1, keepdims=True) for at in range(count)
    ]


def kernel(
    n_gx,
    n_gy,
    beta,
    jump,
    stiff,
    weight,
    owner,
    cell,
    count,
    sol,
    res,
    t_one,
    l_one,
    target,
    lanes_at,
    rim,
    u,
    d,
    invd,
    axl,
    axh,
    ayl,
    ayh,
    azl,
    azh,
    field_t,
    c_one,
    z_high,
    z_low,
    z_at,
    slot_val,
    picked,
    sampled,
    fa_send,
    fa_recv,
    fb_send,
    fb_recv,
    rb_send,
    rb_recv,
    ra_send,
    ra_recv,
    pb_send,
    pb_recv,
    pa_send,
    pa_recv,
    a_ss,
    a_rs,
    b_ss,
    b_rs,
    p_ss,
    p_rs,
    rim_ss,
    rim_rs,
):
    me_x = lax.axis_index("gx")
    me_y = lax.axis_index("gy")
    size_x, size_y, size_z = beta.shape
    rows = jump.shape[0]
    points = rows * LANES
    owners = n_gx * n_gy
    cap = LANES // n_gy
    slots = n_gx * LANES
    columns = size_x * size_y
    chunk = min(CHUNK, slots)
    lane8 = lax.broadcasted_iota(jnp.int32, (PAD, LANES), 1)

    def at_gx(shift):
        return {"gx": lax.rem(me_x + shift + n_gx, n_gx), "gy": me_y}

    def at_gy(shift):
        return {"gx": me_x, "gy": lax.rem(me_y + shift + n_gy, n_gy)}

    def clear(x, _):
        rim[x] = jnp.zeros(rim.shape[1:], F32)
        return 0

    lax.fori_loop(0, rim.shape[0], clear, 0)

    barrier = pltpu.get_barrier_semaphore()

    def greet_x(k, _):
        pl.semaphore_signal(barrier, inc=1, device_id=at_gx(k), device_id_type=MESH)
        return 0

    def greet_y(k, _):
        pl.semaphore_signal(barrier, inc=1, device_id=at_gy(k), device_id_type=MESH)
        return 0

    lax.fori_loop(1, n_gx, greet_x, 0)
    lax.fori_loop(1, n_gy, greet_y, 0)
    for side_x, side_y in SIDES:
        if side_x * side_y:
            corner = {"gx": at_gx(side_x)["gx"], "gy": at_gy(side_y)["gy"]}
            pl.semaphore_signal(barrier, inc=1, device_id=corner, device_id_type=MESH)

    def gx_copy(src, dst, send, recv, k, sign):
        return pltpu.make_async_remote_copy(
            src_ref=src,
            dst_ref=dst,
            send_sem=send,
            recv_sem=recv,
            device_id=at_gx(sign * k),
            device_id_type=MESH,
        )

    def gy_copy(src, dst, send, recv, k, sign):
        return pltpu.make_async_remote_copy(
            src_ref=src,
            dst_ref=dst,
            send_sem=send,
            recv_sem=recv,
            device_id=at_gy(sign * k),
            device_id_type=MESH,
        )

    def wait_for(ref, sem):
        pltpu.make_async_copy(ref, ref, sem).wait()

    def send_gx(src, dst, send, recv, sign):
        def body(k, _):
            gx_copy(src.at[k], dst.at[k], send, recv, k, sign).start()
            return 0

        lax.fori_loop(1, n_gx, body, 0)

    planes = size_x + 2 * DEPTH

    def inside(x, y):
        return (x >= 0) & (x < n_gx) & (y >= 0) & (y < n_gy)

    def rim_copies(f):
        span_x = {
            -1: (DEPTH, DEPTH + size_x, DEPTH),
            0: (DEPTH, DEPTH, size_x),
            1: (size_x, 0, DEPTH),
        }
        span_y = {
            -1: (EDGE, EDGE + size_y, PAD),
            0: (EDGE, EDGE, size_y),
            1: (EDGE + size_y - PAD, EDGE - PAD, PAD),
        }
        for i, (side_x, side_y) in enumerate(SIDES):
            def copy(i=i, side_x=side_x, side_y=side_y, x=span_x[side_x], y=span_y[side_y]):
                return pltpu.make_async_remote_copy(
                    src_ref=rim_part(f, x[0], x[2], y[0], y[2]),
                    dst_ref=rim_part(f, x[1], x[2], y[1], y[2]),
                    send_sem=rim_ss.at[f, i],
                    recv_sem=rim_rs.at[f, i],
                    device_id={"gx": at_gx(side_x)["gx"], "gy": at_gy(side_y)["gy"]},
                    device_id_type=MESH,
                )

            yield (
                inside(me_x + side_x, me_y + side_y),
                inside(me_x - side_x, me_y - side_y),
                copy,
            )

    def rim_part(f, x, count_x, y, count_y):
        return rim.at[pl.ds(f * planes + x, count_x), :, pl.ds(y, count_y), :]

    def rim_send(f):
        for sent, _, copy in rim_copies(f):
            pl.when(sent)(lambda: copy().start())

    def rim_wait(f):
        for _, received, copy in rim_copies(f):
            pl.when(received)(lambda: copy().wait_recv())

    def rim_wait_sent(f):
        for sent, _, copy in rim_copies(f):
            pl.when(sent)(lambda: copy().wait_send())

    shift_gy = n_gy.bit_length() - 1
    own = owner[...]
    target[...] = ((own & (n_gy - 1)) - me_y & (n_gy - 1)) * n_gx + (
        (own >> shift_gy) - me_x & (n_gx - 1)
    )
    iota_t = lax.broadcasted_iota(jnp.int32, (owners, LANES), 0)
    iota_l = lax.broadcasted_iota(jnp.int32, (LANES, LANES), 0)
    above = lax.broadcasted_iota(jnp.int32, (LANES, 2 * LANES), 1)
    below = lax.broadcasted_iota(jnp.int32, (LANES, 2 * LANES), 0)
    counter = ((below < above) | (above >= LANES)).astype(BF16)
    offset = jnp.zeros((owners, LANES), F32)
    for j in range(rows):
        hit = target[j : j + 1, :] == iota_t
        hit_f = jnp.where(hit, 1.0, 0.0)
        hit_b = hit_f.astype(BF16)
        t_one[:, j * LANES : (j + 1) * LANES] = hit_b
        both = nn_dot(hit_b, counter)
        rank = jnp.sum(hit_f * (both[:, :LANES] + offset), axis=0, keepdims=True)
        offset = offset + both[:, LANES:]
        lane_of = rank.astype(jnp.int32) + me_y * cap
        l_one[:, j * LANES : (j + 1) * LANES] = jnp.where(lane_of == iota_l, 1.0, 0.0).astype(BF16)

    def to_rows(vector, row_of):
        out = jnp.zeros((owners, LANES), F32)
        for j in range(rows):
            cols = slice(j * LANES, (j + 1) * LANES)
            for part in row_of(vector[j : j + 1, :]):
                spread = t_one[:, cols] * part
                out = out + nt_dot(spread, l_one[:, cols])
        return out

    def split_index(row):
        low = (row & (2 * LANES - 1)) + 1
        middle = (row >> 8) & (2 * LANES - 1)
        high = row >> 16
        return [
            x.astype(F32).astype(BF16) for x in (low, middle * 256, high * 65536)
        ]

    def forward_a(fields):
        for k in range(n_gy):
            for i, field in enumerate(fields):
                fa_send[k, i * n_gx : (i + 1) * n_gx, :] = field[k * n_gx : (k + 1) * n_gx, :]
        for k in range(1, n_gy):
            gy_copy(fa_send.at[k], fa_recv.at[k], a_ss.at[0], a_rs.at[0], k, 1).start()

    def forward_b():
        wait_for(fa_recv.at[pl.ds(1, n_gy - 1)], a_rs.at[0])
        both = fa_send[0]
        for k in range(1, n_gy):
            both = both + fa_recv[k]
        for k in range(n_gx):
            for i in range(4):
                fb_send[k, i : i + 1, :] = both[i * n_gx + k : i * n_gx + k + 1, :]
        send_gx(fb_send, fb_recv, b_ss.at[0], b_rs.at[0], 1)
        fb_recv[0] = fb_send[0]

    def forward_c():
        wait_for(fb_recv.at[pl.ds(1, n_gx - 1)], b_rs.at[0])
        return [fb_recv[:, i, :] for i in range(4)]

    def back_a(first, second, sums):
        for k in range(n_gx):
            rb_send[k, 0:1, :] = first[k : k + 1, :]
            rb_send[k, 1:2, :] = second[k : k + 1, :]
            rb_send[k, 2:3, :] = sums
            rb_send[k, 3:4, :] = sums
        send_gx(rb_send, rb_recv, b_ss.at[1], b_rs.at[1], -1)
        rb_recv[0] = rb_send[0]

    def back_b():
        wait_for(rb_recv.at[pl.ds(1, n_gx - 1)], b_rs.at[1])
        ra_send[0:n_gx, :] = rb_recv[:, 0, :]
        ra_send[n_gx : 2 * n_gx, :] = rb_recv[:, 1, :]
        sums = jnp.sum(rb_recv[:, 2, :], axis=0, keepdims=True)
        ra_send[2 * n_gx : 2 * n_gx + PAD, :] = jnp.broadcast_to(sums, (PAD, LANES))
        for k in range(1, n_gy):
            gy_copy(ra_send, ra_recv.at[k], a_ss.at[1], a_rs.at[1], k, -1).start()

    def back_c():
        wait_for(ra_recv.at[pl.ds(1, n_gy - 1)], a_rs.at[1])
        blocks = [ra_send[...]] + [ra_recv[k] for k in range(1, n_gy)]
        sums = blocks[0][2 * n_gx : 2 * n_gx + 1, :]
        for b in blocks[1:]:
            sums = sums + b[2 * n_gx : 2 * n_gx + 1, :]
        high, low = halves(
            jnp.concatenate(
                [b[i * n_gx : (i + 1) * n_gx, :] for i in range(2) for b in blocks], axis=0
            )
        )
        for j in range(rows):
            cols = slice(j * LANES, (j + 1) * LANES)
            lanes = l_one[:, cols]
            found = nn_dot(high, lanes) + nn_dot(low, lanes)
            hits = t_one[:, cols].astype(F32)
            for i in range(2):
                sampled[i, j : j + 1, :] = jnp.sum(
                    found[i * owners : (i + 1) * owners, :] * hits, axis=0, keepdims=True
                )
        return sampled[0], sampled[1], sums

    def sum_a(partial):
        pb_send[...] = jnp.broadcast_to(partial, pb_send.shape)

        def body(k, _):
            gx_copy(pb_send, pb_recv.at[k], p_ss.at[0], p_rs.at[0], k, 1).start()
            return 0

        lax.fori_loop(1, n_gx, body, 0)
        pb_recv[0] = pb_send[...]

    def sum_b():
        wait_for(pb_recv.at[pl.ds(1, n_gx - 1)], p_rs.at[0])
        pa_send[...] = jnp.sum(pb_recv[...], axis=0)
        for k in range(1, n_gy):
            gy_copy(pa_send, pa_recv.at[k], p_ss.at[1], p_rs.at[1], k, 1).start()
        pa_recv[0] = pa_send[...]

    def sum_c():
        wait_for(pa_recv.at[pl.ds(1, n_gy - 1)], p_rs.at[1])
        return jnp.sum(pa_recv[...], axis=0)[0:1, :]

    live = lax.broadcasted_iota(jnp.int32, (rows, LANES), 0) < count[...]
    rhs = jnp.where(live, jump[...], 0.0)
    steady = stiff[...]
    sw = jnp.where(live, weight[...], 0.0)
    fields = [to_rows(cell[...], split_index)] + [to_rows(x, halves) for x in (rhs, steady, sw)]
    pl.semaphore_wait(barrier, n_gx + n_gy + 2)
    forward_a(fields)

    def place(x, _):
        for h in range(2):
            rim[DEPTH + x, h, EDGE : EDGE + size_y, :] = beta[x, :, h * LANES : (h + 1) * LANES]
        return 0

    lax.fori_loop(0, size_x, place, 0)
    rim_send(0)
    forward_b()

    def rows_at(ref, x, h, start, n):
        return ref[x, h, pl.ds(start, n), :]

    def z_sides(low, high, lane):
        low_up, high_up = pltpu.roll(low, 1, 1), pltpu.roll(high, 1, 1)
        low_dn, high_dn = pltpu.roll(low, LANES - 1, 1), pltpu.roll(high, LANES - 1, 1)
        return (
            (low_up, jnp.where(lane == 0, low_up, high_up)),
            (jnp.where(lane == LANES - 1, high_dn, low_dn), high_dn),
        )

    def harmonic(a, b):
        both = a + b
        return 2.0 * a * b / jnp.where(both > 0, both, 1.0)

    rim_wait(0)

    def coefficients(x, y):
        row = y + PAD
        centre = [rows_at(rim, x + 1, h, row, PAD) for h in range(2)]
        before, after = z_sides(centre[0], centre[1], lane8)
        for h in range(2):
            c = centre[h]
            kxl = harmonic(c, rows_at(rim, x, h, row, PAD))
            kxh = harmonic(c, rows_at(rim, x + 2, h, row, PAD))
            kyl = harmonic(c, rows_at(rim, x + 1, h, row - 1, PAD))
            kyh = harmonic(c, rows_at(rim, x + 1, h, row + 1, PAD))
            kzl = harmonic(c, before[h])
            kzh = harmonic(c, after[h])
            if h == 0:
                kzl = jnp.where(lane8 == 0, 0.0, kzl)
            else:
                kzh = jnp.where(lane8 == LANES - 1, 0.0, kzh)
            inverse = 1.0 / (SHIFT + kxl + kxh + kyl + kyh + kzl + kzh)
            at = (x, h, pl.ds(y, PAD), slice(None))
            invd[at] = inverse
            axl[at] = kxl * inverse
            axh[at] = kxh * inverse
            ayl[at] = kyl * inverse
            ayh[at] = kyh * inverse
            azl[at] = kzl * inverse
            azh[at] = kzh * inverse

    def coefficient_planes(i, _):
        for x in range(2):
            for y in range(0, size_y + 2 * PAD, PAD):
                coefficients(2 * i + x, y)
        return 0

    lax.fori_loop(0, planes // 2 - 1, coefficient_planes, 0)

    index, slot_rhs, slot_steady, slot_sw = forward_c()
    index = index.astype(jnp.int32) - 1
    z_at[...] = jnp.where(index < 0, -1, index & (size_z - 1))
    slot_val[...] = index >> 8
    iota_c = lax.broadcasted_iota(jnp.int32, (columns, LANES), 0)
    per = chunk // LANES
    iota_z = lax.broadcasted_iota(jnp.int32, (size_z, LANES), 0)
    for j in range(n_gx):
        row = slot_val[j : j + 1, :]
        c_one[:, j * LANES : (j + 1) * LANES] = jnp.where(row == iota_c, 1.0, 0.0).astype(BF16)

    def spread_grid(f, values):
        picked[...] = values
        for j in range(n_gx):
            row = picked[j : j + 1, :]
            hit = z_at[j : j + 1, :] == iota_z
            high = row.astype(BF16).astype(F32)
            cols = slice(j * LANES, (j + 1) * LANES)
            z_high[:, cols] = jnp.where(hit, high, 0.0).astype(BF16)
            z_low[:, cols] = jnp.where(hit, row - high, 0.0).astype(BF16)
        group = 4

        def body(i, _):
            cols = c_one[pl.ds(i * group * size_y, group * size_y), :]
            source = nt_dot(cols, z_high[...]) + nt_dot(cols, z_low[...])
            for q in range(group):
                x = i * group + q
                for h in range(2):
                    part = source[q * size_y : (q + 1) * size_y, h * LANES : (h + 1) * LANES]
                    rim[f * planes + DEPTH + x, h, EDGE : EDGE + size_y, :] = (
                        part * invd[DEPTH - 1 + x, h, PAD : PAD + size_y, :]
                    )
            return 0

        lax.fori_loop(0, size_x // group, body, 0)

    def sample_grid(p):
        def turn(x, _):
            for h in range(2):
                high, low = halves(u[p, DEPTH + x, h, EDGE : EDGE + size_y, :].T)
                field_t[x, h * LANES : (h + 1) * LANES, :] = high
                field_t[x, size_z + h * LANES : size_z + (h + 1) * LANES, :] = low
            return 0

        lax.fori_loop(0, size_x, turn, 0)
        whole = jnp.concatenate([field_t[x] for x in range(size_x)], axis=1)

        def body(i, _):
            found = nn_dot(whole, c_one[:, pl.ds(pl.multiple_of(i * chunk, LANES), chunk)])
            for q in range(per):
                j = i * per + q
                hit = z_at[pl.ds(j, 1), :] == iota_z
                cols = slice(q * LANES, (q + 1) * LANES)
                both = found[:size_z, cols] + found[size_z:, cols]
                picked[pl.ds(j, 1), :] = jnp.sum(
                    jnp.where(hit, both, 0.0), axis=0, keepdims=True
                )
            return 0

        lax.fori_loop(0, slots // chunk, body, 0)

    def relax(f, step, x, y, n, first, second):
        lane = lax.broadcasted_iota(jnp.int32, (n, LANES), 1)
        row = y + PAD

        def field(x, h, row):
            if step == 0:
                return rim[f * planes + x, h, pl.ds(row, n), :]
            return u[(step - 1) % 2, x, h, pl.ds(row, n), :]

        centre = [field(x, h, row) for h in range(2)]
        before, after = z_sides(centre[0], centre[1], lane)
        for h in range(2):
            at = (x - 1, h, pl.ds(y, n), slice(None))
            sides = axl[at] * field(x - 1, h, row) + axh[at] * field(x + 1, h, row)
            sides += ayl[at] * field(x, h, row - 1) + ayh[at] * field(x, h, row + 1)
            sides += azl[at] * before[h] + azh[at] * after[h]
            if step == 0:
                now = centre[h] * (1.0 / THETA)
                update = first * now + second * (centre[h] + (sides - centre[h]) * (1.0 / THETA))
            else:
                now = centre[h]
                update = first * d[at] + second * (rim[f * planes + x, h, pl.ds(row, n), :] + sides - now)
            d[at] = update
            u[step % 2, x, h, pl.ds(row, n), :] = now + update

    def pressure(f):
        rim_send(f)
        rim_wait(f)
        for step, (first, second) in enumerate(sweep_factors()):
            more = CHEB - 2 - step
            low, high = (0, size_y + 2 * PAD) if more else (PAD, size_y + PAD)
            count = size_x + 2 * more
            parts = PARTS if count % PARTS == 0 else 2

            def body(i, _):
                for q in range(count // parts):
                    x = DEPTH - more + i * (count // parts) + q
                    for y in range(low, high, (high - low) // 2):
                        relax(f, step, x, y, (high - low) // 2, first, second)
                return 0

            lax.fori_loop(0, parts, body, 0)
        return (CHEB - 2) % 2

    spread_grid(1, slot_sw * slot_rhs)
    sample_grid(pressure(1))
    got_1 = picked[...]
    slot_a = slot_steady * slot_rhs + slot_sw * got_1
    sum_a(pack_row([total(slot_rhs * slot_rhs), total(slot_rhs * slot_a)]))
    spread_grid(2, slot_sw * slot_a)
    sum_b()
    end = pressure(2)
    sum_bb, sum_ab = unpack_row(sum_c(), 2)
    sample_grid(end)
    got_2 = picked[...]
    start = jnp.sqrt(sum_bb + EPS)
    scale = 1.0 / start
    h_11 = sum_ab * scale * scale

    def basis(first, image, image_of_image):
        v_1 = first * scale
        w_1 = image * scale
        return v_1, w_1, w_1 - h_11 * v_1, image_of_image * scale - h_11 * w_1

    v_1, _, z, s_z = basis(slot_rhs, slot_a, slot_steady * slot_a + slot_sw * got_2)
    pairs = ((z, z), (s_z, v_1), (s_z, z), (s_z, s_z), (v_1, v_1), (v_1, z))
    back_a(got_1, got_2, pack_row([total(p * q) for p, q in pairs]))
    back_b()
    got_1, got_2, sums = back_c()
    image_1 = steady * rhs + sw * got_1
    v_1, w_1, z, s_z = basis(rhs, image_1, jnp.where(live, steady, 0.0) * image_1 + sw * got_2)
    zz, szv, szz, szsz, v1v1, v1z = unpack_row(sums, 6)
    h_21 = jnp.sqrt(zz + EPS)
    inverse = 1.0 / h_21
    v_2 = z * inverse
    w_2 = s_z * inverse
    w2v1, w2v2, w2w2 = szv * inverse, szz * inverse * inverse, szsz * inverse * inverse
    v1v2, v2v2 = v1z * inverse, zz * inverse * inverse
    h_12 = w2v1
    h_22 = w2v2 - h_12 * v1v2
    square = (
        w2w2
        + h_12 * h_12 * v1v1
        + h_22 * h_22 * v2v2
        - 2.0 * h_12 * w2v1
        - 2.0 * h_22 * w2v2
        + 2.0 * h_12 * h_22 * v1v2
    )
    h_32 = jnp.sqrt(jnp.maximum(square, 0.0) + EPS)
    y_1, y_2 = least_squares(start, [[h_11, h_21], [h_12, h_22, h_32]])
    sol[...] = y_1 * v_1 + y_2 * v_2
    res[...] = rhs - y_1 * w_1 - y_2 * w_2

    for f in range(3):
        rim_wait_sent(f)
    wait_for(fa_send.at[pl.ds(1, n_gy - 1)], a_ss.at[0])
    wait_for(ra_recv.at[pl.ds(1, n_gy - 1)], a_ss.at[1])
    wait_for(fb_send.at[pl.ds(1, n_gx - 1)], b_ss.at[0])
    wait_for(rb_send.at[pl.ds(1, n_gx - 1)], b_ss.at[1])
    wait_for(pb_recv.at[pl.ds(1, n_gx - 1)], p_ss.at[0])
    wait_for(pa_recv.at[pl.ds(1, n_gy - 1)], p_ss.at[1])


def on_device(n_gx, n_gy, beta, jump, stiff, weight, owner, cell, count):
    size_x, size_y, size_z = beta.shape
    points = jump.shape[0]
    rows = points // LANES
    owners = n_gx * n_gy
    columns = size_x * size_y
    planes = size_x + 2 * DEPTH
    wide = (planes, 2, size_y + 4 * PAD, LANES)
    tile = (planes - 2, 2, size_y + 2 * PAD, LANES)
    slots = n_gx * LANES
    dma = pltpu.SemaphoreType.DMA
    scratch = [
        pltpu.VMEM((owners, points), BF16),
        pltpu.VMEM((LANES, points), BF16),
        pltpu.VMEM((rows, LANES), jnp.int32),
        pltpu.VMEM((rows, LANES), jnp.int32),
        pltpu.VMEM((3 * planes,) + wide[1:], F32),
        pltpu.VMEM((2,) + wide, F32),
        pltpu.VMEM(tile, F32),
        pltpu.VMEM(tile, F32),
        pltpu.VMEM(tile, F32),
        pltpu.VMEM(tile, F32),
        pltpu.VMEM(tile, F32),
        pltpu.VMEM(tile, F32),
        pltpu.VMEM(tile, F32),
        pltpu.VMEM(tile, F32),
        pltpu.VMEM((size_x, 2 * size_z, size_y), BF16),
        pltpu.VMEM((columns, slots), BF16),
        pltpu.VMEM((size_z, slots), BF16),
        pltpu.VMEM((size_z, slots), BF16),
        pltpu.VMEM((n_gx, LANES), jnp.int32),
        pltpu.VMEM((n_gx, LANES), jnp.int32),
        pltpu.VMEM((n_gx, LANES), F32),
        pltpu.VMEM((2, rows, LANES), F32),
        pltpu.VMEM((n_gy, 4 * n_gx, LANES), F32),
        pltpu.VMEM((n_gy, 4 * n_gx, LANES), F32),
        pltpu.VMEM((n_gx, 4, LANES), F32),
        pltpu.VMEM((n_gx, 4, LANES), F32),
        pltpu.VMEM((n_gx, 4, LANES), F32),
        pltpu.VMEM((n_gx, 4, LANES), F32),
        pltpu.VMEM((2 * n_gx + PAD, LANES), F32),
        pltpu.VMEM((n_gy, 2 * n_gx + PAD, LANES), F32),
        pltpu.VMEM((2, LANES), F32),
        pltpu.VMEM((n_gx, 2, LANES), F32),
        pltpu.VMEM((2, LANES), F32),
        pltpu.VMEM((n_gy, 2, LANES), F32),
    ] + [dma((2,))] * 6 + [dma((3, len(SIDES)))] * 2
    vmem = pl.BlockSpec(memory_space=pltpu.VMEM)
    out = jax.ShapeDtypeStruct((rows, LANES), F32)
    solution, residual = pl.pallas_call(
        functools.partial(kernel, n_gx, n_gy),
        out_shape=(out, out),
        in_specs=[vmem] * 7,
        out_specs=(vmem, vmem),
        scratch_shapes=scratch,
        compiler_params=pltpu.CompilerParams(
            collective_id=0, has_side_effects=True, vmem_limit_bytes=56 * 1024 * 1024
        ),
    )(
        beta,
        jump.reshape(rows, LANES),
        stiff.reshape(rows, LANES),
        weight.reshape(rows, LANES),
        owner.reshape(rows, LANES),
        cell.reshape(rows, LANES),
        count.reshape(1, 1),
    )
    return solution.reshape(points), residual.reshape(points)


def solution(mesh):
    points = P(("gx", "gy"))
    return jax.shard_map(
        functools.partial(on_device, mesh.shape["gx"], mesh.shape["gy"]),
        mesh=mesh,
        in_specs=(P("gx", "gy", None), points, points, points, P(("gx", "gy"), None), points, points),
        out_specs=(points, points),
        check_vma=False,
    )
```

time: 131 us -> 102 us (0.78)
  Pallas kernels: 128 us -> 98.9 us
    pallas_call x1, Pallas kernels: 128 us -> 98.9 us  [on_device(): pl.pallas_call(functools.partial(kernel, n_gx, n_gy), out_shape=(out, out...]
where the time goes in v3:
time: 102 us
  Pallas kernels  98.9 us (97%)
  local copies, waits for them, and re-layouts  1.9 us (2%)
  between operations  1.3 us (1%)
    pallas_call x1, Pallas kernels, on_device(): pl.pallas_call(functools.partial(kernel, n_gx, n_gy), out_shape=(out, out...  98.9 us

profile of v3, /device:TPU:1, one launch (start us, length us, event | category | flops | bytes accessed | tf_op | source)
XLA Modules:
  0.0 102.1 jit_solution(15505013776991268925)
XLA Ops:
  1.3 98.9 %shard_map.86 = (f32[16,128]{1,0:T(8,128)}, f32[16,128]{1,0:T(8,128)}) custom-call(f32[16,64,256]{2,1,0:T(8,128)} %beta.1, f32[16,128]{1,0:T(8,128)} %bitcast.9, f32[16,128]{1,0:T(8,128)} %bitcast.10, f32[16,128]{1,0:T(8,128)} %bitcast.11, s32[16,128]{1,0:T(8,128)} %bitcast.12, s32[16,128]{1,0:T(8,128)} %bitcast.13, s32[1,1]{1,0:T(1,128)} %bitcast.8.count), custom_call_target="tpu_custom_call" | custom-call | tf_op jit(solution)/shard_map/pallas_call | solution.py:679
  100.2 0.0 copy-start
  100.2 1.3 %copy.12 = f32[2048]{0:T(1024)} copy(f32[2048]{0:T(1024)} %bitcast.15) | data formatting | bytes 16384
  101.5 0.0 copy-done
  101.5 0.6 copy.13
Async XLA Ops:
  100.2 1.3 %copy-start = (f32[16,128]{1,0:T(8,128)S(1)}, f32[16,128]{1,0:T(8,128)}, u32[]{:S(2)}) copy-start(f32[16,128]{1,0:T(8,128)} %get-tuple-element.5) | copy-start | bytes 24580

commit v4 on v3

--- a/solution.py
+++ b/solution.py
@@ -16,7 +16,6 @@
 LANES = 128
 PAD = 8
 EDGE = 2 * PAD
-PARTS = 2
 DEPTH = CHEB - 1
 SIDES = [(x, y) for x in (-1, 0, 1) for y in (-1, 0, 1) if (x, y) != (0, 0)]
 MESH = pl.DeviceIdType.MESH
@@ -125,10 +124,10 @@
     ayh,
     azl,
     azh,
+    field_c,
     field_t,
     c_one,
-    z_high,
-    z_low,
+    z_both,
     z_at,
     slot_val,
     picked,
@@ -172,11 +171,25 @@
     def at_gy(shift):
         return {"gx": me_x, "gy": lax.rem(me_y + shift + n_gy, n_gy)}
 
-    def clear(x, _):
-        rim[x] = jnp.zeros(rim.shape[1:], F32)
-        return 0
-
-    lax.fori_loop(0, rim.shape[0], clear, 0)
+    planes = size_x + 2 * DEPTH
+
+    def clear_planes(first):
+        for f in range(3):
+            for x in range(DEPTH):
+                at = f * planes + first + x
+                rim[at] = jnp.zeros(rim.shape[1:], F32)
+
+    def clear_rows(first):
+        def body(x, _):
+            rim[x, :, first : first + EDGE, :] = jnp.zeros((2, EDGE, LANES), F32)
+            return 0
+
+        lax.fori_loop(0, rim.shape[0], body, 0)
+
+    pl.when(me_x == 0)(lambda: clear_planes(0))
+    pl.when(me_x == n_gx - 1)(lambda: clear_planes(size_x + DEPTH))
+    pl.when(me_y == 0)(lambda: clear_rows(0))
+    pl.when(me_y == n_gy - 1)(lambda: clear_rows(EDGE + size_y))
 
     barrier = pltpu.get_barrier_semaphore()
 
@@ -224,8 +237,6 @@
             return 0
 
         lax.fori_loop(1, n_gx, body, 0)
-
-    planes = size_x + 2 * DEPTH
 
     def inside(x, y):
         return (x >= 0) & (x < n_gx) & (y >= 0) & (y < n_gy)
@@ -261,17 +272,26 @@
     def rim_part(f, x, count_x, y, count_y):
         return rim.at[pl.ds(f * planes + x, count_x), :, pl.ds(y, count_y), :]
 
-    def rim_send(f):
-        for sent, _, copy in rim_copies(f):
-            pl.when(sent)(lambda: copy().start())
-
-    def rim_wait(f):
-        for _, received, copy in rim_copies(f):
-            pl.when(received)(lambda: copy().wait_recv())
+    def rim_send(f, along_x=(True, False)):
+        for (side_x, _), (sent, _, copy) in zip(SIDES, rim_copies(f)):
+            if (side_x != 0) in along_x:
+                pl.when(sent)(lambda: copy().start())
+
+    def rim_wait(f, along_x=(True, False)):
+        for (side_x, _), (_, received, copy) in zip(SIDES, rim_copies(f)):
+            if (side_x != 0) in along_x:
+                pl.when(received)(lambda: copy().wait_recv())
 
     def rim_wait_sent(f):
         for sent, _, copy in rim_copies(f):
             pl.when(sent)(lambda: copy().wait_send())
+
+    def place(x, _):
+        for h in range(2):
+            rim[DEPTH + x, h, EDGE : EDGE + size_y, :] = beta[x, :, h * LANES : (h + 1) * LANES]
+        return 0
+
+    lax.fori_loop(0, size_x, place, 0)
 
     shift_gy = n_gy.bit_length() - 1
     own = owner[...]
@@ -399,18 +419,10 @@
     rhs = jnp.where(live, jump[...], 0.0)
     steady = stiff[...]
     sw = jnp.where(live, weight[...], 0.0)
+    pl.semaphore_wait(barrier, n_gx + n_gy + 2)
+    rim_send(0)
     fields = [to_rows(cell[...], split_index)] + [to_rows(x, halves) for x in (rhs, steady, sw)]
-    pl.semaphore_wait(barrier, n_gx + n_gy + 2)
     forward_a(fields)
-
-    def place(x, _):
-        for h in range(2):
-            rim[DEPTH + x, h, EDGE : EDGE + size_y, :] = beta[x, :, h * LANES : (h + 1) * LANES]
-        return 0
-
-    lax.fori_loop(0, size_x, place, 0)
-    rim_send(0)
-    forward_b()
 
     def rows_at(ref, x, h, start, n):
         return ref[x, h, pl.ds(start, n), :]
@@ -461,13 +473,31 @@
                 coefficients(2 * i + x, y)
         return 0
 
-    lax.fori_loop(0, planes // 2 - 1, coefficient_planes, 0)
+    half = (planes // 2 - 1) // 2
+    lax.fori_loop(0, half, coefficient_planes, 0)
+    forward_b()
+    lax.fori_loop(half, planes // 2 - 1, coefficient_planes, 0)
 
     index, slot_rhs, slot_steady, slot_sw = forward_c()
     index = index.astype(jnp.int32) - 1
     z_at[...] = jnp.where(index < 0, -1, index & (size_z - 1))
     slot_val[...] = index >> 8
-    iota_c = lax.broadcasted_iota(jnp.int32, (columns, LANES), 0)
+    near = list(range(DEPTH)) + list(range(size_x - DEPTH, size_x))
+    middle = range(DEPTH, size_x - DEPTH)
+    runs = [
+        [(x, 0, size_y) for x in near[:DEPTH]],
+        [(x, 0, size_y) for x in near[DEPTH:]],
+        [(x, y, PAD) for x in middle for y in (0, size_y - PAD)],
+        [(x, PAD, size_y - 2 * PAD) for x in middle],
+    ]
+    iota_c = jnp.concatenate(
+        [
+            lax.broadcasted_iota(jnp.int32, (n, LANES), 0) + (x * size_y + y)
+            for group in runs
+            for x, y, n in group
+        ],
+        axis=0,
+    )
     per = chunk // LANES
     iota_z = lax.broadcasted_iota(jnp.int32, (size_z, LANES), 0)
     for j in range(n_gx):
@@ -481,37 +511,47 @@
             hit = z_at[j : j + 1, :] == iota_z
             high = row.astype(BF16).astype(F32)
             cols = slice(j * LANES, (j + 1) * LANES)
-            z_high[:, cols] = jnp.where(hit, high, 0.0).astype(BF16)
-            z_low[:, cols] = jnp.where(hit, row - high, 0.0).astype(BF16)
-        group = 4
+            z_both[:size_z, cols] = jnp.where(hit, high, 0.0).astype(BF16)
+            z_both[size_z:, cols] = jnp.where(hit, row - high, 0.0).astype(BF16)
+        at = 0
+        for i, group in enumerate(runs):
+            count = sum(n for _, _, n in group)
+            found = nt_dot(c_one[at : at + count, :], z_both[...])
+            source = found[:, :size_z] + found[:, size_z:]
+            at += count
+            row = 0
+            for x, y, n in group:
+                for h in range(2):
+                    rim[f * planes + DEPTH + x, h, EDGE + y : EDGE + y + n, :] = (
+                        source[row : row + n, h * LANES : (h + 1) * LANES]
+                        * invd[DEPTH - 1 + x, h, PAD + y : PAD + y + n, :]
+                    )
+                row += n
+            if i == 1:
+                rim_send(f, (True,))
+            if i == 2:
+                rim_send(f, (False,))
+
+    def sample_grid(p):
+        at = 0
+        for group in runs:
+            for x, y, n in group:
+                for h in range(2):
+                    field_c[at : at + n, h * LANES : (h + 1) * LANES] = u[
+                        p, DEPTH + x, h, EDGE + y : EDGE + y + n, :
+                    ]
+                at += n
+        for i in range(columns // LANES):
+            cols = slice(i * LANES, (i + 1) * LANES)
+            for h in range(2):
+                high, low = halves(field_c[cols, h * LANES : (h + 1) * LANES].T)
+                field_t[h * LANES : (h + 1) * LANES, cols] = high
+                field_t[size_z + h * LANES : size_z + (h + 1) * LANES, cols] = low
 
         def body(i, _):
-            cols = c_one[pl.ds(i * group * size_y, group * size_y), :]
-            source = nt_dot(cols, z_high[...]) + nt_dot(cols, z_low[...])
-            for q in range(group):
-                x = i * group + q
-                for h in range(2):
-                    part = source[q * size_y : (q + 1) * size_y, h * LANES : (h + 1) * LANES]
-                    rim[f * planes + DEPTH + x, h, EDGE : EDGE + size_y, :] = (
-                        part * invd[DEPTH - 1 + x, h, PAD : PAD + size_y, :]
-                    )
-            return 0
-
-        lax.fori_loop(0, size_x // group, body, 0)
-
-    def sample_grid(p):
-        def turn(x, _):
-            for h in range(2):
-                high, low = halves(u[p, DEPTH + x, h, EDGE : EDGE + size_y, :].T)
-                field_t[x, h * LANES : (h + 1) * LANES, :] = high
-                field_t[x, size_z + h * LANES : size_z + (h + 1) * LANES, :] = low
-            return 0
-
-        lax.fori_loop(0, size_x, turn, 0)
-        whole = jnp.concatenate([field_t[x] for x in range(size_x)], axis=1)
-
-        def body(i, _):
-            found = nn_dot(whole, c_one[:, pl.ds(pl.multiple_of(i * chunk, LANES), chunk)])
+            found = nn_dot(
+                field_t[...], c_one[:, pl.ds(pl.multiple_of(i * chunk, LANES), chunk)]
+            )
             for q in range(per):
                 j = i * per + q
                 hit = z_at[pl.ds(j, 1), :] == iota_z
@@ -550,22 +590,26 @@
             u[step % 2, x, h, pl.ds(row, n), :] = now + update
 
     def pressure(f):
-        rim_send(f)
-        rim_wait(f)
-        for step, (first, second) in enumerate(sweep_factors()):
-            more = CHEB - 2 - step
-            low, high = (0, size_y + 2 * PAD) if more else (PAD, size_y + PAD)
-            count = size_x + 2 * more
-            parts = PARTS if count % PARTS == 0 else 2
-
-            def body(i, _):
-                for q in range(count // parts):
-                    x = DEPTH - more + i * (count // parts) + q
-                    for y in range(low, high, (high - low) // 2):
-                        relax(f, step, x, y, (high - low) // 2, first, second)
+        rim_wait(f, (False,))
+        factors = sweep_factors()
+
+        def step_planes(step, start, count):
+            low, high = (0, size_y + 2 * PAD) if step < CHEB - 2 else (PAD, size_y + PAD)
+            n = (high - low) // 2
+            for x in range(count):
+                for y in (low, low + n):
+                    relax(f, step, start + x, y, n, *factors[step])
+
+        for step in range(CHEB - 1):
+            step_planes(step, DEPTH + step + 1, size_x - 2 * (step + 1))
+        rim_wait(f, (True,))
+        for step in range(CHEB - 1):
+
+            def body(side, _):
+                step_planes(step, step + 1 + side * (planes - DEPTH - 2 * (step + 1)), DEPTH)
                 return 0
 
-            lax.fori_loop(0, parts, body, 0)
+            lax.fori_loop(0, 2, body, 0)
         return (CHEB - 2) % 2
 
     spread_grid(1, slot_sw * slot_rhs)
@@ -653,10 +697,10 @@
         pltpu.VMEM(tile, F32),
         pltpu.VMEM(tile, F32),
         pltpu.VMEM(tile, F32),
-        pltpu.VMEM((size_x, 2 * size_z, size_y), BF16),
+        pltpu.VMEM((columns, size_z), F32),
+        pltpu.VMEM((2 * size_z, columns), BF16),
         pltpu.VMEM((columns, slots), BF16),
-        pltpu.VMEM((size_z, slots), BF16),
-        pltpu.VMEM((size_z, slots), BF16),
+        pltpu.VMEM((2 * size_z, slots), BF16),
         pltpu.VMEM((n_gx, LANES), jnp.int32),
         pltpu.VMEM((n_gx, LANES), jnp.int32),
         pltpu.VMEM((n_gx, LANES), F32),

time: 102 us -> 89.7 us (0.88)
  Pallas kernels: 98.9 us -> 86.3 us
    pallas_call x1, Pallas kernels: 98.9 us -> 86.3 us  [on_device(): pl.pallas_call(functools.partial(kernel, n_gx, n_gy), out_shape=(out, out...]
where the time goes in v4:
time: 89.7 us; the launch traced here: 89.5 us
  Pallas kernels  86.3 us (96%)
  local copies, waits for them, and re-layouts  1.9 us (2%)
  between operations  1.3 us (1%)
    pallas_call x1, Pallas kernels, on_device(): pl.pallas_call(functools.partial(kernel, n_gx, n_gy), out_shape=(out, out...  86.3 us
    unnamed x4, local copies, waits for them, and re-layouts  1.9 us

profile of v4, /device:TPU:1, one launch (start us, length us, event | category | flops | bytes accessed | tf_op | source)
XLA Modules:
  0.0 89.5 jit_solution(15773377471614297105)
XLA Ops:
  1.3 86.3 %shard_map.86 = (f32[16,128]{1,0:T(8,128)}, f32[16,128]{1,0:T(8,128)}) custom-call(f32[16,64,256]{2,1,0:T(8,128)} %beta.1, f32[16,128]{1,0:T(8,128)} %bitcast.9, f32[16,128]{1,0:T(8,128)} %bitcast.10, f32[16,128]{1,0:T(8,128)} %bitcast.11, s32[16,128]{1,0:T(8,128)} %bitcast.12, s32[16,128]{1,0:T(8,128)} %bitcast.13, s32[1,1]{1,0:T(1,128)} %bitcast.8.count), custom_call_target="tpu_custom_call" | custom-call | tf_op jit(solution)/shard_map/pallas_call | solution.py:723
  87.6 0.0 copy-start
  87.6 1.3 %copy.12 = f32[2048]{0:T(1024)} copy(f32[2048]{0:T(1024)} %bitcast.15) | data formatting | bytes 16384
  88.9 0.0 copy-done
  88.9 0.6 copy.13
Async XLA Ops:
  87.6 1.3 %copy-start = (f32[16,128]{1,0:T(8,128)S(1)}, f32[16,128]{1,0:T(8,128)}, u32[]{:S(2)}) copy-start(f32[16,128]{1,0:T(8,128)} %get-tuple-element.5) | copy-start | bytes 24580

commit v5 on v4

--- a/solution.py
+++ b/solution.py
@@ -21,7 +21,7 @@
 MESH = pl.DeviceIdType.MESH
 F32 = jnp.float32
 BF16 = jnp.bfloat16
-CHUNK = 512
+CHUNK = 1024
 
 
 def sweep_factors():
@@ -315,13 +315,31 @@
         lane_of = rank.astype(jnp.int32) + me_y * cap
         l_one[:, j * LANES : (j + 1) * LANES] = jnp.where(lane_of == iota_l, 1.0, 0.0).astype(BF16)
 
-    def to_rows(vector, row_of):
-        out = jnp.zeros((owners, LANES), F32)
-        for j in range(rows):
-            cols = slice(j * LANES, (j + 1) * LANES)
-            for part in row_of(vector[j : j + 1, :]):
-                spread = t_one[:, cols] * part
-                out = out + nt_dot(spread, l_one[:, cols])
+    def to_rows(parts_of):
+        stack = columns // owners
+        parts = 0
+        sizes = []
+        for vector, split in parts_of:
+            for j in range(rows):
+                at = slice(j * LANES, (j + 1) * LANES)
+                rows_j = split(vector[j : j + 1, :])
+                for q, part in enumerate(rows_j):
+                    tall, wide = (parts + q) % stack, (parts + q) // stack
+                    c_one[
+                        tall * owners : (tall + 1) * owners,
+                        wide * points + j * LANES : wide * points + (j + 1) * LANES,
+                    ] = t_one[:, at] * part
+            sizes.append(len(rows_j))
+            parts += len(rows_j)
+        found = []
+        for wide in range(-(-parts // stack)):
+            tall = min(stack, parts - wide * stack) * owners
+            sums = nt_dot(c_one[:tall, wide * points : (wide + 1) * points], l_one[...])
+            found += [sums[q : q + owners, :] for q in range(0, tall, owners)]
+        out = []
+        for size in sizes:
+            out.append(functools.reduce(lambda p, q: p + q, found[:size]))
+            found = found[size:]
         return out
 
     def split_index(row):
@@ -419,10 +437,10 @@
     rhs = jnp.where(live, jump[...], 0.0)
     steady = stiff[...]
     sw = jnp.where(live, weight[...], 0.0)
+    fields = to_rows([(cell[...], split_index)] + [(x, halves) for x in (rhs, steady, sw)])
     pl.semaphore_wait(barrier, n_gx + n_gy + 2)
+    forward_a(fields)
     rim_send(0)
-    fields = [to_rows(cell[...], split_index)] + [to_rows(x, halves) for x in (rhs, steady, sw)]
-    forward_a(fields)
 
     def rows_at(ref, x, h, start, n):
         return ref[x, h, pl.ds(start, n), :]
@@ -438,8 +456,6 @@
     def harmonic(a, b):
         both = a + b
         return 2.0 * a * b / jnp.where(both > 0, both, 1.0)
-
-    rim_wait(0)
 
     def coefficients(x, y):
         row = y + PAD
@@ -467,16 +483,29 @@
             azl[at] = kzl * inverse
             azh[at] = kzh * inverse
 
-    def coefficient_planes(i, _):
-        for x in range(2):
+    ends = planes - 2 - DEPTH
+
+    def inner_planes(rows_of):
+        def body(i, _):
+            for x in range(2):
+                for y in rows_of:
+                    coefficients(DEPTH + 2 * i + x, y)
+            return 0
+
+        lax.fori_loop(0, (ends - DEPTH) // 2, body, 0)
+
+    def end_planes(i, _):
+        for x in (i, ends + i):
             for y in range(0, size_y + 2 * PAD, PAD):
-                coefficients(2 * i + x, y)
+                coefficients(x, y)
         return 0
 
-    half = (planes // 2 - 1) // 2
-    lax.fori_loop(0, half, coefficient_planes, 0)
+    inner_planes(range(2 * PAD, size_y, PAD))
     forward_b()
-    lax.fori_loop(half, planes // 2 - 1, coefficient_planes, 0)
+    rim_wait(0, (False,))
+    inner_planes((0, PAD, size_y, size_y + PAD))
+    rim_wait(0, (True,))
+    lax.fori_loop(0, DEPTH, end_planes, 0)
 
     index, slot_rhs, slot_steady, slot_sw = forward_c()
     index = index.astype(jnp.int32) - 1

time: 89.7 us -> 85.5 us (0.953)
  Pallas kernels: 86.3 us -> 82.2 us
    pallas_call x1, Pallas kernels: 86.3 us -> 82.2 us  [on_device(): pl.pallas_call(functools.partial(kernel, n_gx, n_gy), out_shape=(out, out...]
where the time goes in v5:
time: 85.5 us; the launch traced here: 85.4 us
  Pallas kernels  82.2 us (96%)
  local copies, waits for them, and re-layouts  1.9 us (2%)
  between operations  1.3 us (2%)
    pallas_call x1, Pallas kernels, on_device(): pl.pallas_call(functools.partial(kernel, n_gx, n_gy), out_shape=(out, out...  82.2 us
    unnamed x4, local copies, waits for them, and re-layouts  1.9 us

profile of v5, /device:TPU:1, one launch (start us, length us, event | category | flops | bytes accessed | tf_op | source)
XLA Modules:
  0.0 85.4 jit_solution(13690918818794800148)
XLA Ops:
  1.3 82.2 %shard_map.86 = (f32[16,128]{1,0:T(8,128)}, f32[16,128]{1,0:T(8,128)}) custom-call(f32[16,64,256]{2,1,0:T(8,128)} %beta.1, f32[16,128]{1,0:T(8,128)} %bitcast.9, f32[16,128]{1,0:T(8,128)} %bitcast.10, f32[16,128]{1,0:T(8,128)} %bitcast.11, s32[16,128]{1,0:T(8,128)} %bitcast.12, s32[16,128]{1,0:T(8,128)} %bitcast.13, s32[1,1]{1,0:T(1,128)} %bitcast.8.count), custom_call_target="tpu_custom_call" | custom-call | tf_op jit(solution)/shard_map/pallas_call | solution.py:752
  83.4 0.0 copy-start
  83.5 1.3 %copy.12 = f32[2048]{0:T(1024)} copy(f32[2048]{0:T(1024)} %bitcast.15) | data formatting | bytes 16384
  84.8 0.0 copy-done
  84.8 0.6 copy.13
Async XLA Ops:
  83.4 1.3 %copy-start = (f32[16,128]{1,0:T(8,128)S(1)}, f32[16,128]{1,0:T(8,128)}, u32[]{:S(2)}) copy-start(f32[16,128]{1,0:T(8,128)} %get-tuple-element.5) | copy-start | bytes 24580

commit v6 on v5

--- a/solution.py
+++ b/solution.py
@@ -528,10 +528,13 @@
         axis=0,
     )
     per = chunk // LANES
+    iota_16 = iota_c.astype(jnp.int16)
     iota_z = lax.broadcasted_iota(jnp.int32, (size_z, LANES), 0)
     for j in range(n_gx):
         row = slot_val[j : j + 1, :]
-        c_one[:, j * LANES : (j + 1) * LANES] = jnp.where(row == iota_c, 1.0, 0.0).astype(BF16)
+        c_one[:, j * LANES : (j + 1) * LANES] = jnp.where(
+            row.astype(jnp.int16) == iota_16, jnp.ones((), BF16), jnp.zeros((), BF16)
+        )
 
     def spread_grid(f, values):
         picked[...] = values

time: 85.5 us -> 84.2 us (0.985)
  Pallas kernels: 82.2 us -> 80.8 us
    pallas_call x1, Pallas kernels: 82.2 us -> 80.8 us  [on_device(): pl.pallas_call(functools.partial(kernel, n_gx, n_gy), out_shape=(out, out...]
where the time goes in v6:
time: 84.2 us; the launch traced here: 84 us
  Pallas kernels  80.8 us (96%)
  local copies, waits for them, and re-layouts  1.9 us (2%)
  between operations  1.3 us (2%)
    pallas_call x1, Pallas kernels, on_device(): pl.pallas_call(functools.partial(kernel, n_gx, n_gy), out_shape=(out, out...  80.8 us
    unnamed x4, local copies, waits for them, and re-layouts  1.9 us

profile of v6, /device:TPU:1, one launch (start us, length us, event | category | flops | bytes accessed | tf_op | source)
XLA Modules:
  0.0 84.0 jit_solution(360806609598971400)
XLA Ops:
  1.3 80.8 %shard_map.86 = (f32[16,128]{1,0:T(8,128)}, f32[16,128]{1,0:T(8,128)}) custom-call(f32[16,64,256]{2,1,0:T(8,128)} %beta.1, f32[16,128]{1,0:T(8,128)} %bitcast.9, f32[16,128]{1,0:T(8,128)} %bitcast.10, f32[16,128]{1,0:T(8,128)} %bitcast.11, s32[16,128]{1,0:T(8,128)} %bitcast.12, s32[16,128]{1,0:T(8,128)} %bitcast.13, s32[1,1]{1,0:T(1,128)} %bitcast.8.count), custom_call_target="tpu_custom_call" | custom-call | tf_op jit(solution)/shard_map/pallas_call | solution.py:755
  82.1 0.0 copy-start
  82.1 1.3 %copy.12 = f32[2048]{0:T(1024)} copy(f32[2048]{0:T(1024)} %bitcast.15) | data formatting | bytes 16384
  83.4 0.0 copy-done
  83.4 0.6 copy.13
Async XLA Ops:
  82.1 1.3 %copy-start = (f32[16,128]{1,0:T(8,128)S(1)}, f32[16,128]{1,0:T(8,128)}, u32[]{:S(2)}) copy-start(f32[16,128]{1,0:T(8,128)} %get-tuple-element.5) | copy-start | bytes 24580
